TPU v7x, 32 devices: a whole 2x2x4 slice. The times are simulated.
32 devices in a mesh: groups: 2 (over x), owner: 8 (over z, y), dp: 2 (over core).
Axes of the slice: x: 2, y: 2, z: 4, core: 2. Of those that a mesh axis runs over, the one named last changes fastest.
Arguments:
- activations: bfloat16 [4, 16, 28672], P(('groups', 'dp'), 'owner'), parts along dimension 0, may hold values from -6 to 6
- out_grads: bfloat16 [4, 16, 8192], P(('groups', 'dp'), 'owner'), parts along dimension 0, may hold values from -6 to 6
- lengths: int32 [4, 4], P('groups'), parts along dimension 0, may hold values from 1 to 8, 16 in all within a row
- rollout_ids: int32 [16], P('groups'), parts along dimension 0, may hold values from 0 to 7, each once
- basis_in: bfloat16 [28672, 16384], P(None, ('owner', 'dp')), may hold values from -0.03125 to 0.03125
- basis_out: bfloat16 [8192, 8192], P(None, ('owner', 'dp')), may hold values from -0.0625 to 0.0625
- eigvals: bfloat16 [8192, 16384], P(None, ('owner', 'dp')), may hold values from 0.049804688 to 5
- query_out: bfloat16 [128, 8, 8192], P(None, None, ('owner', 'dp')), may hold values from -0.0078125 to 0.0078125
- query_in: bfloat16 [128, 8, 16384], P(None, None, ('owner', 'dp')), may hold values from -0.005859375 to 0.005859375
- query_ids: int32 [64], P('groups'), parts along dimension 0, may hold values from 0 to 127
Outputs:
- influence: float32 [16, 32], P('groups'), parts along dimension 0
There are 2 independent parts, one for each index of `groups`. A program takes and returns all parts, laid end to end along the dimension named above; an argument that names none is the same for every part. Nothing has to cross between parts.
Inputs may be any that keep to these rules, and one draw needn't show every extreme that they name: Each replica's lengths sum to 16, and its longest rollout has exactly 8 tokens. `rollout_ids`: each rollout number appears once.
All inputs are finite; a program needn't handle non-finite values.
Results may differ from a plain program's by a relative error of at most 0.005.
Values may be sent and summed in bfloat16 or wider, within the bound.
A program may use at most 256 MiB of HBM per device.

v0:
```python
import jax
import jax.numpy as jnp
from jax import lax
from jax.sharding import PartitionSpec as P

DAMPING = 0.1


def rotate_rows(piece, basis):
    flat = piece.reshape(-1, piece.shape[-1])
    turned = jnp.dot(flat, basis, preferred_element_type=jnp.float32).astype(jnp.bfloat16)
    return turned.reshape(piece.shape[:-1] + (basis.shape[1],))


def replica_scores(rot_in, rot_out, inv_eig, sel_full, sel_cols, lengths_row, queries):
    sel_wide = sel_cols.astype(jnp.float32)
    columns = rot_in.shape[1]
    slots = rot_in.shape[0]
    window = slots // 2
    ends = jnp.cumsum(lengths_row)
    starts = ends - lengths_row

    def per_rollout(bounds):
        begin_at, end_at = bounds
        offset = jnp.minimum(begin_at, slots - window)
        rows_in = lax.dynamic_slice_in_dim(rot_in, offset, window, 0)
        rows_out = lax.dynamic_slice_in_dim(rot_out, offset, window, 0)
        position = offset + jnp.arange(window, dtype=jnp.int32)
        inside = ((position >= begin_at) & (position < end_at)).astype(rot_in.dtype)
        masked = rows_in * inside[:, None]
        outer_sum = lax.dot_general(
            rows_out, masked, (((0,), (0,)), ((), ())), preferred_element_type=jnp.float32
        )
        scaled = (outer_sum * inv_eig).astype(jnp.bfloat16)
        projected = jnp.dot(sel_full, scaled, preferred_element_type=jnp.float32)
        return jnp.sum((projected * sel_wide).reshape(queries, -1, columns), axis=(1, 2))

    return lax.map(per_rollout, (starts, ends))


def on_device(
    activations,
    out_grads,
    lengths,
    rollout_ids,
    basis_in,
    basis_out,
    eigvals,
    query_out,
    query_in,
    query_ids,
):
    queries = query_ids.shape[0]
    bank = query_out.shape[0]
    slots = activations.shape[1]
    owners = lax.axis_size("owner")
    replicas = lax.axis_size("dp")
    per_replica = lengths.shape[1]
    rollouts = rollout_ids.shape[0]
    picker = (query_ids[:, None] == jnp.arange(bank, dtype=jnp.int32)[None, :]).astype(jnp.bfloat16)
    sel_out = jnp.einsum(
        "qb,brj->qrj", picker, query_out, preferred_element_type=jnp.float32
    ).astype(jnp.bfloat16)
    sel_out = sel_out.reshape(queries * sel_out.shape[1], -1)
    sel_in = jnp.einsum("qb,brk->qrk", picker, query_in, preferred_element_type=jnp.float32).astype(
        jnp.bfloat16
    )
    sel_in = sel_in.reshape(queries * sel_in.shape[1], -1)
    sel_full = lax.all_gather(sel_out, ("owner", "dp"), axis=1, tiled=True)
    targets = jnp.arange(rollouts, dtype=jnp.int32)
    id_table = rollout_ids.reshape(replicas, per_replica)
    inv_eig = 1.0 / (eigvals.astype(jnp.float32) + DAMPING)
    all_in = rotate_rows(
        lax.all_gather(activations, ("owner", "dp"), axis=1, tiled=True), basis_in
    )[0]
    block_out = rotate_rows(
        lax.all_gather(out_grads, ("owner", "dp"), axis=1, tiled=True), basis_out
    )
    all_out = lax.all_gather(block_out, ("owner", "dp"), axis=2, tiled=True)[0]
    partial_value = jnp.zeros((rollouts, queries), jnp.float32)
    for replica in range(replicas):
        rows_in = all_in.reshape(owners, replicas, slots, -1)[:, replica].reshape(
            owners * slots, -1
        )
        rows_out = all_out.reshape(owners, replicas, slots, -1)[:, replica].reshape(
            owners * slots, -1
        )
        scores = replica_scores(
            rows_in, rows_out, inv_eig, sel_full, sel_in, lengths[replica], queries
        )
        placing = (id_table[replica][:, None] == targets[None, :]).astype(jnp.float32)
        partial_value = partial_value + jnp.einsum("ep,eq->pq", placing, scores)
    return lax.psum(partial_value, ("owner", "dp"))


def solution(mesh):
    return jax.shard_map(
        on_device,
        mesh=mesh,
        in_specs=(
            P(("groups", "dp"), "owner", None),
            P(("groups", "dp"), "owner", None),
            P("groups", None),
            P("groups"),
            P(None, ("owner", "dp")),
            P(None, ("owner", "dp")),
            P(None, ("owner", "dp")),
            P(None, None, ("owner", "dp")),
            P(None, None, ("owner", "dp")),
            P("groups"),
        ),
        out_specs=P("groups", None),
        check_vma=False,
    )
```

profile of v0, /device:TPU:0, one launch (start us, length us, event | category | flops | bytes accessed | tf_op | source)
XLA Modules:
  0.0 314.2 jit_solution(11834745307655962213)
XLA Ops:
  6.6 1.9 copy.28
  8.6 2.0 convolution_convert_fusion
  10.5 0.8 copy.58
  11.4 0.8 copy.27
  12.2 27.6 %all_gather.12 = bf16[1,32,8192]{2,0,1:T(2,128)(2,1)S(1)} all-gather(bf16[1,2,8192]{2,0,1:T(2,128)(2,1)S(1)} %copy.27), channel_id=1, replica_groups=mesh['groups'=2,'owner'=8,'dp'=2] {'owner','dp'}, dimensions={1}, use_global_device_ids=true | all-gather | bytes 557056 | tf_op jit(solution)/shard_map/all_gather | solution.py:77
  39.8 5.4 %convolution_convert_fusion.1 = bf16[32,512]{1,0:T(8,128)(2,1)S(1)} fusion(bf16[8192,512]{1,0:T(8,128)(2,1)} %param.19, bf16[1,32,8192]{2,0,1:T(2,128)(2,1)S(1)} %all_gather.12), kind=kOutput, calls=%fused_computation.34 | convolution fusion | flops 268451840 | bytes 8945664 | tf_op jit(solution)/shard_map/dot_general | solution.py:11
  45.2 21.0 %all-gather = bf16[32,8192]{1,0:T(8,128)(2,1)S(1)} all-gather(bf16[32,512]{1,0:T(8,128)(2,1)S(1)} %convolution_convert_fusion.1), channel_id=2, replica_groups=mesh['groups'=2,'owner'=8,'dp'=2] {'owner','dp'}, dimensions={1}, use_global_device_ids=true | all-gather | bytes 557056 | tf_op jit(solution)/shard_map/all_gather | solution.py:79
  66.3 0.3 reshape_squeeze.16
  66.6 0.4 fusion.57
  67.0 0.2 reduce-window.19
  67.2 0.2 reduce-window.18
  67.4 0.1 reshape_squeeze.19
  67.5 0.1 reshape_squeeze.17
  67.6 2.4 fusion.40
  70.0 0.6 copy.57
  70.6 0.3 copy.33
  71.1 19.0 %add_divide_fusion = f32[8192,1024]{1,0:T(8,128)} fusion(bf16[8192,1024]{1,0:T(8,128)(2,1)} %param.20), kind=kLoop, calls=%fused_computation.24 | loop fusion | flops 25165824 | bytes 50331648 | tf_op jit(solution)/shard_map/div | solution.py:72
  90.1 23.2 %fusion.43 = bf16[32,1024]{1,0:T(8,128)(2,1)S(1)} fusion(bf16[28672,1024]{1,0:T(8,128)(2,1)} %param.18, bf16[1,32,28672]{2,0,1:T(2,128)(2,1)} %all-gather.4.cloned.1.call-done), kind=kOutput, calls=%fused_computation.33 | convolution fusion | flops 1879080960 | bytes 60620800 | tf_op jit(solution)/shard_map/dot_general | solution.py:11
  113.4 7.5 %all-gather.6.cloned.1.call-done = bf16[256,8192]{1,0:T(8,128)(2,1)} async-done(((bf16[256,512]{1,0:T(8,128)(2,1)}), bf16[256,8192]{1,0:T(8,128)(2,1)}) %all-gather.6.cloned.1.call-update) | async-done | bytes 4194320 | tf_op jit(solution)/shard_map/all_gather | solution.py:69
  121.0 77.2 %while.21 = (s32[]{:T(128)}, bf16[4,32]{1,0:T(4,128)(2,1)S(1)}, s32[4]{0:T(128)S(1)}, bf16[16,8192]{1,0:T(8,128)(2,1)S(1)}, bf16[16,1024]{1,0:T(8,128)(2,1)S(1)}...) while((s32[]{:T(128)}, bf16[4,32]{1,0:T(4,128)(2,1)S(1)}, ...), condition=%wide.region_9.10_spmd, body=%wide.region_6.9_spmd.sunk | while | flops 4446519296 | bytes 38950840 | solution.py:38
  121.0 0.6 dynamic_slice.55
  122.2 0.6 dynamic_slice.56
  122.8 1.2 and_convert_fusion.5
  124.0 16.0 %fusion.81 = f32[256]{0:T(256)S(1)} fusion(f32[256,1024]{0,1:T(8,128)S(1)} %get-tuple-element.389, bf16[256,8192]{1,0:T(8,128)(2,1)} %get-tuple-element.388, f32[8192,1024]{1,0:T(8,128)} %get-tuple-element.387, bf16[16,8192]{1,0:T(8,128)(2,1)S(1)} %get-tuple-element.384, s32[]{:T(128)S(6)} %select_n.11, ...), kind=kOutput, calls=%fused_computation.17.clone.1 | convolution fusion | flops 4446519296 | bytes 38947328 | tf_op jit(solution)/shard_map/while/body/eval_jaxpr/dot_general | solution.py:35
  140.1 0.1 reduce_sum.45
  140.3 0.6 dynamic_slice.55
  141.5 0.6 dynamic_slice.56
  142.1 1.2 and_convert_fusion.5
  143.3 16.0 %fusion.81 = f32[256]{0:T(256)S(1)} fusion(f32[256,1024]{0,1:T(8,128)S(1)} %get-tuple-element.389, bf16[256,8192]{1,0:T(8,128)(2,1)} %get-tuple-element.388, f32[8192,1024]{1,0:T(8,128)} %get-tuple-element.387, bf16[16,8192]{1,0:T(8,128)(2,1)S(1)} %get-tuple-element.384, s32[]{:T(128)S(6)} %select_n.11, ...), kind=kOutput, calls=%fused_computation.17.clone.1 | convolution fusion | flops 4446519296 | bytes 38947328 | tf_op jit(solution)/shard_map/while/body/eval_jaxpr/dot_general | solution.py:35
  159.4 0.1 reduce_sum.45
  159.6 0.6 dynamic_slice.55
  160.8 0.6 dynamic_slice.56
  161.4 1.2 and_convert_fusion.5
  162.6 16.0 %fusion.81 = f32[256]{0:T(256)S(1)} fusion(f32[256,1024]{0,1:T(8,128)S(1)} %get-tuple-element.389, bf16[256,8192]{1,0:T(8,128)(2,1)} %get-tuple-element.388, f32[8192,1024]{1,0:T(8,128)} %get-tuple-element.387, bf16[16,8192]{1,0:T(8,128)(2,1)S(1)} %get-tuple-element.384, s32[]{:T(128)S(6)} %select_n.11, ...), kind=kOutput, calls=%fused_computation.17.clone.1 | convolution fusion | flops 4446519296 | bytes 38947328 | tf_op jit(solution)/shard_map/while/body/eval_jaxpr/dot_general | solution.py:35
  178.7 0.1 reduce_sum.45
  178.8 0.6 dynamic_slice.55
  180.1 0.6 dynamic_slice.56
  180.7 1.2 and_convert_fusion.5
  181.9 16.0 %fusion.81 = f32[256]{0:T(256)S(1)} fusion(f32[256,1024]{0,1:T(8,128)S(1)} %get-tuple-element.389, bf16[256,8192]{1,0:T(8,128)(2,1)} %get-tuple-element.388, f32[8192,1024]{1,0:T(8,128)} %get-tuple-element.387, bf16[16,8192]{1,0:T(8,128)(2,1)S(1)} %get-tuple-element.384, s32[]{:T(128)S(6)} %select_n.11, ...), kind=kOutput, calls=%fused_computation.17.clone.1 | convolution fusion | flops 4446519296 | bytes 38947328 | tf_op jit(solution)/shard_map/while/body/eval_jaxpr/dot_general | solution.py:35
  198.0 0.1 reduce_sum.45
  198.1 77.2 %while.20 = (s32[]{:T(128)}, bf16[4,32]{1,0:T(4,128)(2,1)S(1)}, s32[4]{0:T(128)S(1)}, bf16[16,8192]{1,0:T(8,128)(2,1)S(1)}, bf16[16,1024]{1,0:T(8,128)(2,1)S(1)}...) while((s32[]{:T(128)}, bf16[4,32]{1,0:T(4,128)(2,1)S(1)}, ...), condition=%wide.region_4.5_spmd, body=%wide.region_1.4_spmd.sunk | while | flops 4446519296 | bytes 38950840 | solution.py:38
  198.2 0.6 dynamic_slice.51
  199.4 0.6 dynamic_slice.52
  200.0 1.2 and_convert_fusion.4
  201.2 16.0 %fusion.77 = f32[256]{0:T(256)S(1)} fusion(f32[256,1024]{0,1:T(8,128)S(1)} %get-tuple-element.347, bf16[256,8192]{1,0:T(8,128)(2,1)} %get-tuple-element.346, f32[8192,1024]{1,0:T(8,128)} %get-tuple-element.345, bf16[16,8192]{1,0:T(8,128)(2,1)S(1)} %get-tuple-element.342, s32[]{:T(128)S(6)} %select_n.10, bf16[16,1024]{1,0:T(8,128)(2,1)S(1)} %get-tuple-element.343, ...), kind=kOutput, calls=%fused_computation.5.clone.1 | convolution fusion | flops 4446519296 | bytes 38947328 | tf_op jit(solution)/shard_map/while/body/eval_jaxpr/dot_general | solution.py:35
  217.3 0.1 reduce_sum.42
  217.5 0.6 dynamic_slice.51
  218.7 0.6 dynamic_slice.52
  219.3 1.2 and_convert_fusion.4
  220.5 16.0 %fusion.77 = f32[256]{0:T(256)S(1)} fusion(f32[256,1024]{0,1:T(8,128)S(1)} %get-tuple-element.347, bf16[256,8192]{1,0:T(8,128)(2,1)} %get-tuple-element.346, f32[8192,1024]{1,0:T(8,128)} %get-tuple-element.345, bf16[16,8192]{1,0:T(8,128)(2,1)S(1)} %get-tuple-element.342, s32[]{:T(128)S(6)} %select_n.10, bf16[16,1024]{1,0:T(8,128)(2,1)S(1)} %get-tuple-element.343, ...), kind=kOutput, calls=%fused_computation.5.clone.1 | convolution fusion | flops 4446519296 | bytes 38947328 | tf_op jit(solution)/shard_map/while/body/eval_jaxpr/dot_general | solution.py:35
  236.6 0.1 reduce_sum.42
  236.8 0.6 dynamic_slice.51
  238.0 0.6 dynamic_slice.52
  238.6 1.2 and_convert_fusion.4
  239.8 16.0 %fusion.77 = f32[256]{0:T(256)S(1)} fusion(f32[256,1024]{0,1:T(8,128)S(1)} %get-tuple-element.347, bf16[256,8192]{1,0:T(8,128)(2,1)} %get-tuple-element.346, f32[8192,1024]{1,0:T(8,128)} %get-tuple-element.345, bf16[16,8192]{1,0:T(8,128)(2,1)S(1)} %get-tuple-element.342, s32[]{:T(128)S(6)} %select_n.10, bf16[16,1024]{1,0:T(8,128)(2,1)S(1)} %get-tuple-element.343, ...), kind=kOutput, calls=%fused_computation.5.clone.1 | convolution fusion | flops 4446519296 | bytes 38947328 | tf_op jit(solution)/shard_map/while/body/eval_jaxpr/dot_general | solution.py:35
  255.9 0.1 reduce_sum.42
  256.0 0.6 dynamic_slice.51
  257.3 0.6 dynamic_slice.52
  257.9 1.2 and_convert_fusion.4
  259.1 16.0 %fusion.77 = f32[256]{0:T(256)S(1)} fusion(f32[256,1024]{0,1:T(8,128)S(1)} %get-tuple-element.347, bf16[256,8192]{1,0:T(8,128)(2,1)} %get-tuple-element.346, f32[8192,1024]{1,0:T(8,128)} %get-tuple-element.345, bf16[16,8192]{1,0:T(8,128)(2,1)S(1)} %get-tuple-element.342, s32[]{:T(128)S(6)} %select_n.10, bf16[16,1024]{1,0:T(8,128)(2,1)S(1)} %get-tuple-element.343, ...), kind=kOutput, calls=%fused_computation.5.clone.1 | convolution fusion | flops 4446519296 | bytes 38947328 | tf_op jit(solution)/shard_map/while/body/eval_jaxpr/dot_general | solution.py:35
  275.2 0.1 reduce_sum.42
  275.3 0.3 fusion.54
  275.6 0.3 convolution_add_fusion
  275.9 31.5 %psum.7 = f32[8,32]{1,0:T(8,128)} all-reduce(f32[8,32]{1,0:T(8,128)S(1)} %convolution_add_fusion), channel_id=1, replica_groups=mesh['groups'=2,'owner'=8,'dp'=2] {'owner','dp'}, use_global_device_ids=true, to_apply=%region_10.11 | all-reduce | flops 256 | bytes 2048 | tf_op jit(solution)/shard_map/psum | solution.py:93
  (40 shorter events, 1.3 us)
Async XLA Ops:
  6.5 61.1 %copy-start = (bf16[128,8,1024]{2,1,0:T(8,128)(2,1)S(1)}, bf16[128,8,1024]{2,1,0:T(8,128)(2,1)}, u32[]{:S(2)}) copy-start(bf16[128,8,1024]{2,1,0:T(8,128)(2,1)} %param.22) | copy-start | bytes 6291460
  6.5 61.1 %copy-start.4 = (s32[32]{0:T(128)S(1)}, s32[32]{0:T(128)}, u32[]{:S(2)}) copy-start(s32[32]{0:T(128)} %param.23) | copy-start | bytes 388
  6.5 60.5 %copy-start.2 = (s32[2,4]{1,0:T(2,128)S(1)}, s32[2,4]{1,0:T(2,128)}, u32[]{:S(2)}) copy-start(s32[2,4]{1,0:T(2,128)} %param.16) | copy-start | bytes 100
  6.5 64.4 %copy-start.3 = (s32[8]{0:T(128)S(1)}, s32[8]{0:T(128)}, u32[]{:S(2)}) copy-start(s32[8]{0:T(128)} %param.17) | copy-start | bytes 100
  6.5 83.5 %all-gather.4.cloned.1.call-start = ((), (), s32[]{:S(2)}) async-start(), calls=%async_computation | async-start | bytes 3899392 | tf_op jit(solution)/shard_map/all_gather | solution.py:74
  8.5 112.4 %all-gather.6.cloned.1.call-start = ((), (), s32[]{:S(2)}) async-start(), calls=%async_computation.1 | async-start | bytes 4456448 | tf_op jit(solution)/shard_map/all_gather | solution.py:69
  275.3 32.0 %copy-start.1 = (bf16[128,8,1024]{2,1,0:T(8,128)(2,1)S(1)}, bf16[128,8,1024]{2,1,0:T(8,128)(2,1)}, u32[]{:S(2)}) copy-start(bf16[128,8,1024]{2,1,0:T(8,128)(2,1)} %param.22) | copy-start | bytes 6291460
Sparse Core Ops, SparseCore 0:
  9.7 57.1 all-gather.3
  69.0 51.8 all-gather.5
where the time goes:
time: 315 us; the launch traced here: 314 us
  matrix products  162 us (51%)
  blocking collectives  80.1 us (25%)
  other arithmetic  29.8 us (9%)
  local copies, waits for them, and re-layouts  16.1 us (5%)
  between operations  13.6 us (4%)
  waiting for transfers between devices  7.57 us (2%)
  loops' own time  5.3 us (2%)
    dot_general x8, matrix products, per_rollout(): projected = jnp.dot(sel_full, scaled, preferred_element_type=jnp.float32)  128 us
    psum x1, blocking collectives, on_device(): return lax.psum(partial_value, ('owner', 'dp'))  31.5 us
    dot_general x2, matrix products, rotate_rows(): jnp.dot(flat, basis, preferred_element_type=jnp.float32)  28.6 us
    all_gather x1, blocking collectives, on_device(): lax.all_gather(out_grads, ('owner', 'dp'), axis=1, tiled=True)  27.6 us
    all_gather x1, blocking collectives, on_device(): all_out = lax.all_gather(block_out, ('owner', 'dp'), axis=2, tiled=True)[0]  21 us
    div x1, other arithmetic, on_device(): inv_eig = 1.0 / (eigvals.astype(jnp.float32) + DAMPING)  19 us
    convert_element_type x8, other arithmetic, per_rollout(): inside = ((position >= begin_at) & (position < end_at)).astype(rot_in.dtype)  9.48 us
    dynamic_slice x16, local copies, waits for them, and re-layouts, replica_scores(): return lax.map(per_rollout, (starts, ends))  9.42 us
  transfers between devices with their start and end apart: 2, of which 1 were waited for; matrix products, arithmetic and copies ran while one was open for 18% of the time, Pallas kernels for 0%

commit v1 on v0

v1 whole, which is shorter than its diff:
```python
import functools

import jax
import jax.numpy as jnp
from jax import lax
from jax.experimental import pallas as pl
from jax.experimental.pallas import tpu as pltpu
from jax.sharding import PartitionSpec as P

DAMPING = 0.1
BOTH = ("owner", "dp")


def score_kernel(rollouts, k_tile, out_ref_t, sel_out_ref, eig_ref, masked_ref, sel_in_ref, acc_ref):
    @pl.when(pl.program_id(0) == 0)
    def _():
        acc_ref[...] = jnp.zeros_like(acc_ref)

    rows, columns = eig_ref.shape
    wide = sel_in_ref.shape[1]
    damped = eig_ref[...].astype(jnp.float32) + DAMPING
    rough = pl.reciprocal(damped, approx=True)
    inv = rough * (2.0 - damped * rough)
    tokens_t = out_ref_t[...]
    sel_out = sel_out_ref[...].astype(jnp.float32)
    for e in range(rollouts):
        turned = jnp.zeros((rows, wide), jnp.float32)
        for at in range(0, columns, k_tile):
            outer = jnp.dot(
                tokens_t, masked_ref[e, :, at : at + k_tile], preferred_element_type=jnp.float32
            )
            scaled = (outer * inv[:, at : at + k_tile]).astype(jnp.bfloat16)
            turned += jnp.dot(
                scaled, sel_in_ref[at : at + k_tile, :], preferred_element_type=jnp.float32
            )
        acc_ref[e] += jnp.sum((turned * sel_out).reshape(rows // 8, 8, wide), axis=0)


def plane_scores(rot_out_t, sel_out_t, eigvals, masked_in, sel_in_t):
    total, columns = eigvals.shape
    rollouts, tokens, _ = masked_in.shape
    wide = sel_in_t.shape[1]
    rows = min(512, total)
    k_tile = min(256, columns)
    return pl.pallas_call(
        functools.partial(score_kernel, rollouts, k_tile),
        grid=(total // rows,),
        in_specs=[
            pl.BlockSpec((rows, tokens), lambda i: (i, 0)),
            pl.BlockSpec((rows, wide), lambda i: (i, 0)),
            pl.BlockSpec((rows, columns), lambda i: (i, 0)),
            pl.BlockSpec((rollouts, tokens, columns), lambda i: (0, 0, 0)),
            pl.BlockSpec((columns, wide), lambda i: (0, 0)),
        ],
        out_specs=pl.BlockSpec((rollouts, 8, wide), lambda i: (0, 0, 0)),
        out_shape=jax.ShapeDtypeStruct((rollouts, 8, wide), jnp.float32),
        compiler_params=pltpu.CompilerParams(vmem_limit_bytes=48 * 1024 * 1024),
        cost_estimate=pl.CostEstimate(
            flops=2 * rollouts * total * columns * (wide + 256),
            bytes_accessed=2 * total * (columns + wide),
            transcendentals=total * columns,
        ),
    )(rot_out_t, sel_out_t, eigvals, masked_in, sel_in_t)


def on_device(
    activations,
    out_grads,
    lengths,
    rollout_ids,
    basis_in,
    basis_out,
    eigvals,
    query_out,
    query_in,
    query_ids,
):
    queries = query_ids.shape[0]
    bank, rank, _ = query_out.shape
    slots = activations.shape[1]
    owners = lax.axis_size("owner")
    replicas = lax.axis_size("dp")
    per_replica = lengths.shape[1]
    rollouts = rollout_ids.shape[0]
    tokens = owners * replicas * slots
    picker = (query_ids[:, None] == jnp.arange(bank, dtype=jnp.int32)[None, :]).astype(jnp.bfloat16)

    grads = lax.all_gather(out_grads[0], BOTH, axis=0, tiled=True)
    acts = lax.all_gather(activations[0], BOTH, axis=0, tiled=True)
    sel_out_t = jnp.einsum(
        "qb,brj->jqr", picker, query_out, preferred_element_type=jnp.float32
    ).astype(jnp.bfloat16)
    sel_out_t = lax.all_gather(sel_out_t.reshape(-1, queries * rank), BOTH, axis=0, tiled=True)
    sel_in_t = jnp.einsum(
        "qb,brk->kqr", picker, query_in, preferred_element_type=jnp.float32
    ).astype(jnp.bfloat16)
    sel_in_t = sel_in_t.reshape(-1, queries * rank)

    block_out = jnp.dot(grads, basis_out, preferred_element_type=jnp.float32).astype(jnp.bfloat16)
    rot_out_t = lax.all_gather(block_out.T, BOTH, axis=0, tiled=True)
    rot_in = jnp.dot(acts, basis_in, preferred_element_type=jnp.float32).astype(jnp.bfloat16)

    token = jnp.arange(tokens, dtype=jnp.int32)
    place = (token // (replicas * slots)) * slots + token % slots
    replica = (token // slots) % replicas
    ends = jnp.cumsum(lengths, axis=1)
    starts = ends - lengths
    member = (
        (jnp.arange(replicas, dtype=jnp.int32)[:, None, None] == replica[None, None, :])
        & (place[None, None, :] >= starts[:, :, None])
        & (place[None, None, :] < ends[:, :, None])
    ).reshape(rollouts, tokens)
    masked_in = jnp.where(member[:, :, None], rot_in[None], jnp.zeros((), rot_in.dtype))

    acc = plane_scores(rot_out_t, sel_out_t, eigvals, masked_in, sel_in_t)
    scores = jnp.sum(acc.reshape(rollouts, 8, queries, rank), axis=(1, 3))
    scores = lax.psum(scores, BOTH)
    placing = (rollout_ids[:, None] == jnp.arange(rollouts, dtype=jnp.int32)[None, :]).astype(
        jnp.float32
    )
    return jnp.sum(placing[:, :, None] * scores[:, None, :], axis=0)


def solution(mesh):
    return jax.shard_map(
        on_device,
        mesh=mesh,
        in_specs=(
            P(("groups", "dp"), "owner", None),
            P(("groups", "dp"), "owner", None),
            P("groups", None),
            P("groups"),
            P(None, BOTH),
            P(None, BOTH),
            P(None, BOTH),
            P(None, None, BOTH),
            P(None, None, BOTH),
            P("groups"),
        ),
        out_specs=P("groups", None),
        check_vma=False,
    )
```

time: 315 us -> 239 us (0.76)
  matrix products: 162 us -> 33.2 us
  Pallas kernels: 0 us -> 78.1 us
  other arithmetic: 29.8 us -> 2.6 us
  blocking collectives: 80.1 us -> 90.3 us
  local copies, waits for them, and re-layouts: 16.1 us -> 6.23 us
  waiting for transfers between devices: 7.57 us -> 14.8 us
  loops' own time: 5.3 us -> 0 us
    dot_general x14 -> x4, matrix products: 162 us -> 33.2 us  [the longest x1 23.1 us: on_device(): jnp.dot(acts, basis_in, preferred_element_type=jnp.float32)]
    pallas_call x0 -> x1, Pallas kernels: none -> 78.1 us  [plane_scores(): pl.pallas_call(functools.partial(score_kernel, rollouts, k_tile), grid=(t...]
    div x1 -> x0, other arithmetic: 19 us -> none  [on_device(): inv_eig = 1.0 / (eigvals.astype(jnp.float32) + DAMPING)]
    all_gather x2, blocking collectives: 48.6 us -> 59.1 us  [the longest x1 31.4 us: on_device(): rot_out_t = lax.all_gather(block_out.T, BOTH, axis=0, tiled=True)]
    dynamic_slice x16 -> x0, local copies, waits for them, and re-layouts: 9.42 us -> none  [replica_scores(): return lax.map(per_rollout, (starts, ends))]
    convert_element_type x8 -> x1, other arithmetic: 9.48 us -> 0.07 us  [on_device(): (rollout_ids[:, None] == jnp.arange(rollouts, dtype=jnp.int32)[None, :])....]
    all_gather x2, waiting for transfers between devices: 7.53 us -> 14.7 us  [the longest x1 14.7 us: on_device(): lax.all_gather(sel_out_t.reshape(-1, queries * rank), BOTH, axis=0, tiled...]
    another operation x2 -> x0, loops' own time: 5.3 us -> none  [replica_scores(): return lax.map(per_rollout, (starts, ends))]
  transfers between devices with their start and end apart: 2 -> 2, of which waited for: 1 -> 1; matrix products, arithmetic and copies ran while one was open for 18% -> 16% of each run, Pallas kernels for 0% -> 0%
where the time goes in v1:
time: 239 us
  blocking collectives  90.3 us (38%)
  Pallas kernels  78.1 us (33%)
  matrix products  33.2 us (14%)
  waiting for transfers between devices  14.8 us (6%)
  between operations  13.5 us (6%)
  local copies, waits for them, and re-layouts  6.23 us (3%)
  other arithmetic  2.6 us (1%)
    pallas_call x1, Pallas kernels, plane_scores(): pl.pallas_call(functools.partial(score_kernel, rollouts, k_tile), grid=(t...  78.1 us
    all_gather x1, blocking collectives, on_device(): rot_out_t = lax.all_gather(block_out.T, BOTH, axis=0, tiled=True)  31.4 us
    psum x1, blocking collectives, on_device(): scores = lax.psum(scores, BOTH)  31.2 us
    all_gather x1, blocking collectives, on_device(): grads = lax.all_gather(out_grads[0], BOTH, axis=0, tiled=True)  27.7 us
    dot_general x1, matrix products, on_device(): jnp.dot(acts, basis_in, preferred_element_type=jnp.float32)  23.1 us
    all_gather x1, waiting for transfers between devices, on_device(): lax.all_gather(sel_out_t.reshape(-1, queries * rank), BOTH, axis=0, tiled...  14.7 us
    dot_general x1, matrix products, on_device(): jnp.dot(grads, basis_out, preferred_element_type=jnp.float32)  5.03 us
  transfers between devices with their start and end apart: 2, of which 1 were waited for; matrix products, arithmetic and copies ran while one was open for 16% of the time, Pallas kernels for 0%

profile of v1, /device:TPU:0, one launch (start us, length us, event | category | flops | bytes accessed | tf_op | source)
XLA Modules:
  0.0 238.8 jit_solution(5844450931565100049)
XLA Ops:
  6.5 0.0 copy-start
  6.5 0.0 all-gather.7.cloned.1.call-start
  6.5 1.9 copy.55
  8.5 0.0 all-gather.7.cloned.1.call-update
  8.5 0.0 all-gather.5.cloned.1.call-start
  8.5 2.0 fusion.11
  10.5 0.2 copy.82
  10.7 0.9 copy.54
  11.5 0.0 all-gather.5.cloned.1.call-update
  11.5 0.9 reduce_window_sum.11
  12.4 0.1 lt.31
  12.5 0.7 sub.17
  13.2 0.1 ge.22
  13.2 0.8 copy.50
  14.0 0.0 copy-done
  14.1 3.1 %fusion.8 = bf16[1024,32,8]{0,1,2:T(8,128)(2,1)S(1)} fusion(bf16[128,8,1024]{2,1,0:T(8,128)(2,1)S(1)} %copy-done, s32[32]{0:T(128)} %param.19), kind=kOutput, calls=%fused_computation.6 | convolution fusion | flops 67375104 | bytes 2621568 | tf_op jit(solution)/shard_map/qb,brk->kqr/dot_general | solution.py:94
  17.1 0.3 copy.81
  17.4 0.2 copy.58.sel_in_ref
  17.6 27.7 %all-gather = bf16[1,32,8192]{2,0,1:T(2,128)(2,1)S(1)} all-gather(bf16[1,2,8192]{2,0,1:T(2,128)(2,1)S(1)} %copy.50), channel_id=2, replica_groups=mesh['groups'=2,'owner'=8,'dp'=2] {'owner','dp'}, dimensions={1}, use_global_device_ids=true | all-gather | bytes 557056 | tf_op jit(solution)/shard_map/all_gather | solution.py:88
  45.4 0.0 copy-start.3
  45.4 5.0 %convolution_convert_fusion.1 = bf16[512,32]{0,1:T(8,128)(2,1)S(1)} fusion(bf16[8192,512]{1,0:T(8,128)(2,1)} %param.15, bf16[1,32,8192]{2,0,1:T(2,128)(2,1)S(1)} %all-gather), kind=kOutput, calls=%fused_computation.10 | convolution fusion | flops 268451840 | bytes 8945664 | tf_op jit(solution)/shard_map/dot_general | solution.py:99
  50.4 0.1 copy.51
  50.6 0.1 compare_and_fusion
  50.7 0.0 copy-done.3
  50.7 0.1 fusion.23
  50.7 31.4 %all_gather.13.out_ref_t = bf16[8192,32]{1,0:T(8,128)(2,1)} all-gather(bf16[512,32]{1,0:T(8,128)(2,1)S(1)} %copy.51), channel_id=1, replica_groups=mesh['groups'=2,'owner'=8,'dp'=2] {'owner','dp'}, dimensions={0}, use_global_device_ids=true | all-gather | bytes 557056 | tf_op jit(solution)/shard_map/all_gather | solution.py:100
  82.1 0.0 all-gather.7.cloned.1.call-done
  82.1 23.1 %fusion.12 = bf16[32,1024]{1,0:T(8,128)(2,1)S(1)} fusion(bf16[28672,1024]{1,0:T(8,128)(2,1)} %param.14, bf16[1,32,28672]{2,0,1:T(2,128)(2,1)} %all-gather.7.cloned.1.call-done), kind=kOutput, calls=%fused_computation.9 | convolution fusion | flops 1879080960 | bytes 60620800 | tf_op jit(solution)/shard_map/dot_general | solution.py:101
  105.3 0.1 broadcast_select_fusion.masked_ref
  105.4 14.7 %all-gather.5.cloned.1.call-done.sel_out_ref = bf16[8192,256]{1,0:T(8,128)(2,1)} async-done(((bf16[512,256]{1,0:T(8,128)(2,1)}), bf16[8192,256]{1,0:T(8,128)(2,1)}) %all-gather.5.cloned.1.call-update) | async-done | bytes 4194320 | tf_op jit(solution)/shard_map/all_gather | solution.py:93
  120.2 0.0 copy-start.2
  120.2 1.6 copy-done.2
  121.8 0.0 copy-start.1
  121.8 78.1 %shard_map.100 = f32[8,8,256]{2,1,0:T(8,128)S(1)} custom-call(bf16[8192,32]{1,0:T(8,128)(2,1)S(1)} %copy-done.2, bf16[8192,256]{1,0:T(8,128)(2,1)} %all-gather.5.cloned.1.call-done.sel_out_ref, bf16[8192,1024]{1,0:T(8,128)(2,1)} %eig_ref.1, bf16[8,32,1024]{2,1,0:T(8,128)(2,1)S(1)} %broadcast_select_fusion.masked_ref, bf16[1024,256]{1,0:T(8,128)(2,1)S(1)} %copy.58.sel_in_ref), custom_call_target="tpu_custom_call" | custom-call | flops 68719476736 | bytes 20971520 | tf_op jit(solution)/shard_map/pallas_call | solution.py:45
  199.9 0.1 reduce_sum.26
  200.0 0.1 reduce_sum.27
  200.1 31.2 %psum.7 = f32[8,32]{1,0:T(8,128)S(1)} all-reduce(f32[8,32]{1,0:T(8,128)S(1)} %reduce_sum.27), channel_id=1, replica_groups=mesh['groups'=2,'owner'=8,'dp'=2] {'owner','dp'}, use_global_device_ids=true, to_apply=%region_3.4 | all-reduce | flops 256 | bytes 2048 | tf_op jit(solution)/shard_map/psum | solution.py:117
  231.3 0.7 multiply_reduce_fusion
  232.0 0.0 copy-done.1
  (5 shorter events, 0.0 us)
Async XLA Ops:
  6.5 7.5 %copy-start = (bf16[128,8,1024]{2,1,0:T(8,128)(2,1)S(1)}, bf16[128,8,1024]{2,1,0:T(8,128)(2,1)}, u32[]{:S(2)}) copy-start(bf16[128,8,1024]{2,1,0:T(8,128)(2,1)} %param.18) | copy-start | bytes 6291460
  6.5 75.6 %all-gather.7.cloned.1.call-start = ((), (), s32[]{:S(2)}) async-start(), calls=%async_computation.1 | async-start | bytes 3899392 | tf_op jit(solution)/shard_map/all_gather | solution.py:89
  8.5 111.7 %all-gather.5.cloned.1.call-start = ((), (), s32[]{:S(2)}) async-start(), calls=%async_computation | async-start | bytes 4456448 | tf_op jit(solution)/shard_map/all_gather | solution.py:93
  45.4 5.3 %copy-start.3 = (s32[8]{0:T(128)S(1)}, s32[8]{0:T(128)}, u32[]{:S(2)}) copy-start(s32[8]{0:T(128)} %param.13) | copy-start | bytes 100
  120.2 1.6 copy-start.2
  121.8 110.2 %copy-start.1 = (bf16[128,8,1024]{2,1,0:T(8,128)(2,1)S(1)}, bf16[128,8,1024]{2,1,0:T(8,128)(2,1)}, u32[]{:S(2)}) copy-start(bf16[128,8,1024]{2,1,0:T(8,128)(2,1)} %param.18) | copy-start | bytes 6291460
Sparse Core Ops, SparseCore 0:
  9.6 58.3 all-gather.6
  70.2 49.9 all-gather.4

commit v2 on v1

--- a/solution.py
+++ b/solution.py
@@ -9,6 +9,100 @@
 
 DAMPING = 0.1
 BOTH = ("owner", "dp")
+
+
+def gather_kernel(lines, along, block_ref, all_ref, send_sem, recv_sem, own_sem):
+    owner, core = lax.axis_index("owner"), lax.axis_index("dp")
+    line, place = owner // along, owner % along
+    cores = lax.axis_size("dp")
+
+    def index(a, b, c):
+        return (a * along + b) * cores + c
+
+    line_peers = [lax.rem(line + s, lines) for s in range(1, lines)]
+    row_peers = [lax.rem(place + s, along) for s in range(1, along)]
+    core_peers = [lax.rem(core + s, cores) for s in range(1, cores)]
+    peers = [(a, place, core) for a in line_peers]
+    peers += [(line, b, core) for b in row_peers]
+    peers += [(line, place, c) for c in core_peers]
+
+    def device(a, b, c):
+        return {"owner": a * along + b, "dp": c}
+
+    barrier = pltpu.get_barrier_semaphore()
+    for peer in peers:
+        pl.semaphore_signal(
+            barrier, inc=1, device_id=device(*peer), device_id_type=pl.DeviceIdType.MESH
+        )
+    pl.semaphore_wait(barrier, len(peers))
+
+    sent = []
+
+    def push(source, slot, peer):
+        copy = pltpu.make_async_remote_copy(
+            src_ref=source,
+            dst_ref=all_ref.at[slot],
+            send_sem=send_sem.at[len(sent)],
+            recv_sem=recv_sem.at[slot],
+            device_id=device(*peer),
+            device_id_type=pl.DeviceIdType.MESH,
+        )
+        copy.start()
+        sent.append(copy)
+
+    def arrived(slot):
+        pltpu.make_async_copy(block_ref, all_ref.at[slot], recv_sem.at[slot]).wait()
+
+    mine = index(line, place, core)
+    for peer in peers:
+        push(block_ref, mine, peer)
+    own = pltpu.make_async_copy(block_ref, all_ref.at[mine], own_sem)
+    own.start()
+    for a in line_peers:
+        slot = index(a, place, core)
+        arrived(slot)
+        for b in row_peers:
+            push(all_ref.at[slot], slot, (line, b, core))
+        for c in core_peers:
+            push(all_ref.at[slot], slot, (line, place, c))
+    for a in [line] + line_peers:
+        for b in row_peers:
+            slot = index(a, b, core)
+            arrived(slot)
+            for c in core_peers:
+                push(all_ref.at[slot], slot, (line, place, c))
+    for c in core_peers:
+        for a in [line] + line_peers:
+            for b in [place] + row_peers:
+                arrived(index(a, b, c))
+    own.wait()
+    for copy in sent:
+        copy.wait_send()
+
+
+def gather_blocks(block, collective_id):
+    owners, cores = lax.axis_size("owner"), lax.axis_size("dp")
+    along = 2 if owners < 16 else 8
+    lines = owners // along
+    copies = lines + along + cores - 3
+    copies += (lines - 1) * (along + cores - 2) + lines * (along - 1) * (cores - 1)
+    return pl.pallas_call(
+        functools.partial(gather_kernel, lines, along),
+        in_specs=[pl.BlockSpec(memory_space=pl.ANY)],
+        out_specs=pl.BlockSpec(memory_space=pl.ANY),
+        out_shape=jax.ShapeDtypeStruct((owners * cores,) + block.shape, block.dtype),
+        scratch_shapes=[
+            pltpu.SemaphoreType.DMA((copies,)),
+            pltpu.SemaphoreType.DMA((owners * cores,)),
+            pltpu.SemaphoreType.DMA,
+        ],
+        compiler_params=pltpu.CompilerParams(
+            collective_id=collective_id, has_side_effects=True
+        ),
+        cost_estimate=pl.CostEstimate(
+            flops=0, bytes_accessed=2 * owners * cores * block.size * 2, transcendentals=0
+        ),
+    )(block)
 
 
 def score_kernel(rollouts, k_tile, out_ref_t, sel_out_ref, eig_ref, masked_ref, sel_in_ref, acc_ref):
@@ -85,8 +179,10 @@
     tokens = owners * replicas * slots
     picker = (query_ids[:, None] == jnp.arange(bank, dtype=jnp.int32)[None, :]).astype(jnp.bfloat16)
 
-    grads = lax.all_gather(out_grads[0], BOTH, axis=0, tiled=True)
-    acts = lax.all_gather(activations[0], BOTH, axis=0, tiled=True)
+    wide_in, wide_out = activations.shape[2], out_grads.shape[2]
+    both = jnp.concatenate(
+        [activations.reshape(-1, 128), out_grads.reshape(-1, 128)], axis=0
+    )
     sel_out_t = jnp.einsum(
         "qb,brj->jqr", picker, query_out, preferred_element_type=jnp.float32
     ).astype(jnp.bfloat16)
@@ -96,8 +192,12 @@
     ).astype(jnp.bfloat16)
     sel_in_t = sel_in_t.reshape(-1, queries * rank)
 
+    gathered = gather_blocks(both, 0)
+    split = slots * wide_in // 128
+    acts = gathered[:, :split].reshape(tokens, wide_in)
+    grads = gathered[:, split:].reshape(tokens, wide_out)
     block_out = jnp.dot(grads, basis_out, preferred_element_type=jnp.float32).astype(jnp.bfloat16)
-    rot_out_t = lax.all_gather(block_out.T, BOTH, axis=0, tiled=True)
+    rot_out_t = gather_blocks(block_out, 1).transpose(0, 2, 1).reshape(-1, tokens)
     rot_in = jnp.dot(acts, basis_in, preferred_element_type=jnp.float32).astype(jnp.bfloat16)
 
     token = jnp.arange(tokens, dtype=jnp.int32)
@@ -114,7 +214,8 @@
 
     acc = plane_scores(rot_out_t, sel_out_t, eigvals, masked_in, sel_in_t)
     scores = jnp.sum(acc.reshape(rollouts, 8, queries, rank), axis=(1, 3))
-    scores = lax.psum(scores, BOTH)
+    shares = gather_blocks(jnp.pad(scores, ((0, 0), (0, -queries % 128))), 2)
+    scores = jnp.sum(shares, axis=0)[:, :queries]
     placing = (rollout_ids[:, None] == jnp.arange(rollouts, dtype=jnp.int32)[None, :]).astype(
         jnp.float32
     )

time: 239 us -> 202 us (0.85)
  blocking collectives: 90.3 us -> 0 us
  Pallas kernels: 78.1 us -> 140 us
  waiting for transfers between devices: 14.8 us -> 0.04 us
  local copies, waits for them, and re-layouts: 6.23 us -> 13.7 us
    pallas_call x0 -> x3, Pallas kernels: none -> 61.9 us  [gather_blocks(): pl.pallas_call(functools.partial(gather_kernel, lines, along), in_specs=[...]
    all_gather x2 -> x0, blocking collectives: 59.1 us -> none  [the longest x1 31.4 us: on_device(): rot_out_t = lax.all_gather(block_out.T, BOTH, axis=0, tiled=True)]
    psum x1 -> x0, blocking collectives: 31.2 us -> none  [on_device(): scores = lax.psum(scores, BOTH)]
    all_gather x1, waiting for transfers between devices: 14.7 us -> 0.02 us  [on_device(): lax.all_gather(sel_out_t.reshape(-1, queries * rank), BOTH, axis=0, tiled...]
    reshape x0 -> x4, local copies, waits for them, and re-layouts: none -> 3.29 us  [the longest x1 2.94 us: on_device(): acts = gathered[:, :split].reshape(tokens, wide_in)]
    slice x0 -> x3, local copies, waits for them, and re-layouts: none -> 2.95 us  [the longest x1 2.94 us: on_device(): acts = gathered[:, :split].reshape(tokens, wide_in)]
    transpose x0 -> x1, local copies, waits for them, and re-layouts: none -> 2.67 us  [on_device(): gather_blocks(block_out, 1).transpose(0, 2, 1).reshape(-1, tokens)]
  transfers between devices with their start and end apart: 2 -> 1, of which waited for: 1 -> 0; matrix products, arithmetic and copies ran while one was open for 16% -> 20% of each run, Pallas kernels for 0% -> 25%
where the time goes in v2:
time: 202 us
  Pallas kernels  140 us (69%)
  matrix products  31.5 us (16%)
  local copies, waits for them, and re-layouts  13.7 us (7%)
  between operations  13.6 us (7%)
  other arithmetic  2.78 us (1%)
    pallas_call x1, Pallas kernels, plane_scores(): pl.pallas_call(functools.partial(score_kernel, rollouts, k_tile), grid=(t...  78.1 us
    pallas_call x3, Pallas kernels, gather_blocks(): pl.pallas_call(functools.partial(gather_kernel, lines, along), in_specs=[...  61.9 us
    dot_general x1, matrix products, on_device(): jnp.dot(acts, basis_in, preferred_element_type=jnp.float32)  21.5 us
    dot_general x1, matrix products, on_device(): jnp.dot(grads, basis_out, preferred_element_type=jnp.float32)  5.54 us
  transfers between devices with their start and end apart: 1, of which 0 were waited for; matrix products, arithmetic and copies ran while one was open for 20% of the time, Pallas kernels for 25%

profile of v2, /device:TPU:0, one launch (start us, length us, event | category | flops | bytes accessed | tf_op | source)
XLA Modules:
  0.0 201.7 jit_solution(3781041891389920681)
XLA Ops:
  6.5 0.0 copy-start
  6.5 0.0 copy-start.6
  6.5 0.0 copy-start.4
  6.5 0.0 copy-start.5
  6.5 0.0 all-gather.2.cloned.1.call-start
  6.6 2.1 %fusion.8 = bf16[512,32,8]{0,1,2:T(8,128)(2,1)S(1)} fusion(bf16[128,8,512]{2,1,0:T(8,128)(2,1)} %param.17, s32[32]{0:T(128)} %param.19), kind=kOutput, calls=%fused_computation.5 | convolution fusion | flops 33689600 | bytes 1310848 | tf_op jit(solution)/shard_map/qb,brj->jqr/dot_general | solution.py:186
  8.7 0.2 copy.41
  8.9 0.9 copy.26
  9.7 0.0 all-gather.2.cloned.1.call-update
  9.7 0.0 copy-done.6
  9.7 0.2 reduce_window_sum.11
  9.9 0.1 lt.31
  10.0 0.0 copy-done.4
  10.0 0.1 reshape.162
  10.1 0.0 copy-done.5
  10.2 0.7 pad_maximum_fusion.block_ref
  10.8 29.1 %shard_map.100 = bf16[16,576,128]{2,1,0:T(8,128)(2,1)} custom-call(bf16[576,128]{1,0:T(8,128)(2,1)} %pad_maximum_fusion.block_ref), custom_call_target="tpu_custom_call" | custom-call | bytes 4718592 | tf_op jit(solution)/shard_map/pallas_call | solution.py:89
  40.0 2.9 %slice.10 = bf16[16,448,128]{2,1,0:T(8,128)(2,1)} slice(bf16[16,576,128]{2,1,0:T(8,128)(2,1)} %shard_map.100), slice={[0:16], [0:448], [0:128]} | slice | bytes 3670016 | tf_op jit(solution)/shard_map/slice | solution.py:197
  42.9 0.0 slice-start
  42.9 0.1 ge.22
  43.0 2.9 %reshape.167 = bf16[32,28672]{1,0:T(8,128)(2,1)} reshape(bf16[16,448,128]{2,1,0:T(8,128)(2,1)} %slice.10) | data formatting | bytes 3670016 | tf_op jit(solution)/shard_map/reshape | solution.py:197
  45.9 0.0 slice-done
  45.9 0.2 reshape.164
  46.1 5.5 %convolution_convert_fusion.2.block_ref = bf16[32,512]{1,0:T(8,128)(2,1)} fusion(bf16[32,8192]{1,0:T(8,128)(2,1)S(1)} %reshape.164, bf16[8192,512]{1,0:T(8,128)(2,1)} %param.15), kind=kOutput, calls=%fused_computation.7 | convolution fusion | flops 268451840 | bytes 8945664 | tf_op jit(solution)/shard_map/dot_general | solution.py:199
  51.7 0.0 copy-start.7
  51.7 20.4 %shard_map.101 = bf16[16,32,512]{2,1,0:T(8,128)(2,1)} custom-call(bf16[32,512]{1,0:T(8,128)(2,1)} %convolution_convert_fusion.2.block_ref), custom_call_target="tpu_custom_call" | custom-call | bytes 1048576 | tf_op jit(solution)/shard_map/pallas_call | solution.py:89
  72.1 2.7 %copy.23 = bf16[16,512,32]{2,1,0:T(8,128)(2,1)} copy(bf16[16,512,32]{1,2,0:T(8,128)(2,1)} %bitcast.23) | data formatting | bytes 1048576 | tf_op jit(solution)/shard_map/transpose | solution.py:200
  74.8 0.0 copy-done
  74.8 0.0 copy-done.7
  74.8 0.0 copy-start.8
  74.8 2.4 %fusion.5 = bf16[1024,32,8]{0,1,2:T(8,128)(2,1)S(1)} fusion(bf16[128,8,1024]{2,1,0:T(8,128)(2,1)S(1)} %copy-done, s32[32]{0:T(128)S(1)} %copy-done.7), kind=kOutput, calls=%fused_computation.3 | convolution fusion | flops 67375104 | bytes 2621568 | tf_op jit(solution)/shard_map/qb,brk->kqr/dot_general | solution.py:190
  77.2 0.0 copy-start.3
  77.2 0.3 copy.40
  77.5 0.2 copy.29.sel_in_ref
  77.8 0.1 compare_and_fusion
  77.9 0.0 copy-done.8
  77.9 0.1 fusion.15
  77.9 0.8 copy-done.3
  78.7 21.5 %convolution_convert_fusion.1 = bf16[32,1024]{1,0:T(8,128)(2,1)S(1)} fusion(bf16[32,28672]{1,0:T(8,128)(2,1)S(1)} %copy-done.3, bf16[28672,1024]{1,0:T(8,128)(2,1)} %param.14), kind=kOutput, calls=%fused_computation.6 | convolution fusion | flops 1879080960 | bytes 60620800 | tf_op jit(solution)/shard_map/dot_general | solution.py:201
  100.2 0.1 broadcast_select_fusion.masked_ref
  100.3 0.0 all-gather.2.cloned.1.call-done.sel_out_ref
  100.4 0.0 copy-start.2
  100.4 1.6 copy-done.2
  102.0 0.0 copy-start.1
  102.0 78.1 %shard_map.102 = f32[8,8,256]{2,1,0:T(8,128)S(1)} custom-call(bf16[8192,32]{1,0:T(8,128)(2,1)S(1)} %bitcast.22, bf16[8192,256]{1,0:T(8,128)(2,1)} %all-gather.2.cloned.1.call-done.sel_out_ref, bf16[8192,1024]{1,0:T(8,128)(2,1)} %eig_ref.1, bf16[8,32,1024]{2,1,0:T(8,128)(2,1)S(1)} %broadcast_select_fusion.masked_ref, bf16[1024,256]{1,0:T(8,128)(2,1)S(1)} %copy.29.sel_in_ref), custom_call_target="tpu_custom_call" | custom-call | flops 68719476736 | bytes 20971520 | tf_op jit(solution)/shard_map/pallas_call | solution.py:139
  180.1 0.1 reduce_sum.35
  180.2 0.1 reduce_sum.36
  180.3 0.6 pad.4.block_ref
  180.9 12.3 %shard_map.103 = f32[16,8,128]{2,1,0:T(8,128)} custom-call(f32[8,128]{1,0:T(8,128)} %pad.4.block_ref), custom_call_target="tpu_custom_call" | custom-call | bytes 65536 | tf_op jit(solution)/shard_map/pallas_call | solution.py:89
  193.3 0.9 reduce_sum.37
  194.1 0.7 multiply_reduce_fusion
  194.8 0.0 copy-done.1
  (7 shorter events, 0.1 us)
Async XLA Ops:
  6.5 68.3 %copy-start = (bf16[128,8,1024]{2,1,0:T(8,128)(2,1)S(1)}, bf16[128,8,1024]{2,1,0:T(8,128)(2,1)}, u32[]{:S(2)}) copy-start(bf16[128,8,1024]{2,1,0:T(8,128)(2,1)} %param.18) | copy-start | bytes 6291460
  6.5 3.2 %copy-start.6 = (s32[2,4]{1,0:T(2,128)S(1)}, s32[2,4]{1,0:T(2,128)}, u32[]{:S(2)}) copy-start(s32[2,4]{1,0:T(2,128)} %param.12) | copy-start | bytes 100
  6.5 3.5 %copy-start.4 = (bf16[1,2,28672]{2,1,0:T(2,128)(2,1)S(1)}, bf16[1,2,28672]{2,1,0:T(2,128)(2,1)}, u32[]{:S(2)}) copy-start(bf16[1,2,28672]{2,1,0:T(2,128)(2,1)} %param.10) | copy-start | bytes 344068
  6.5 3.6 %copy-start.5 = (bf16[1,2,8192]{2,1,0:T(2,128)(2,1)S(1)}, bf16[1,2,8192]{2,1,0:T(2,128)(2,1)}, u32[]{:S(2)}) copy-start(bf16[1,2,8192]{2,1,0:T(2,128)(2,1)} %param.11) | copy-start | bytes 98308
  6.5 93.8 %all-gather.2.cloned.1.call-start = ((), (), s32[]{:S(2)}) async-start(), calls=%async_computation | async-start | bytes 4456448 | tf_op jit(solution)/shard_map/all_gather | solution.py:189
  42.9 3.0 %slice-start = ((bf16[16,576,128]{2,1,0:T(8,128)(2,1)}), bf16[16,128,128]{2,1,0:T(8,128)(2,1)S(1)}, s32[]{:S(2)}) async-start(bf16[16,576,128]{2,1,0:T(8,128)(2,1)} %shard_map.100), calls=%async_computation.1 | async-start | bytes 1048576 | tf_op jit(solution)/shard_map/slice | solution.py:198
  51.7 23.1 %copy-start.7 = (s32[32]{0:T(128)S(1)}, s32[32]{0:T(128)}, u32[]{:S(2)}) copy-start(s32[32]{0:T(128)} %param.19) | copy-start | bytes 388
  74.8 3.1 %copy-start.8 = (s32[8]{0:T(128)S(1)}, s32[8]{0:T(128)}, u32[]{:S(2)}) copy-start(s32[8]{0:T(128)} %param.13) | copy-start | bytes 100
  77.2 1.5 copy-start.3
  100.4 1.6 copy-start.2
  102.0 92.9 %copy-start.1 = (bf16[128,8,1024]{2,1,0:T(8,128)(2,1)S(1)}, bf16[128,8,1024]{2,1,0:T(8,128)(2,1)}, u32[]{:S(2)}) copy-start(bf16[128,8,1024]{2,1,0:T(8,128)(2,1)} %param.18) | copy-start | bytes 6291460
Sparse Core Ops, SparseCore 0:
  9.9 62.0 all-gather.1

commit v3 on v2

v3 whole, which is shorter than its diff:
```python
import functools

import jax
import jax.numpy as jnp
from jax import lax
from jax.experimental import pallas as pl
from jax.experimental.pallas import tpu as pltpu
from jax.sharding import PartitionSpec as P

DAMPING = 0.1
BOTH = ("owner", "dp")


def gather_kernel(lines, along, arrays, *refs):
    blocks, alls = refs[:arrays], refs[arrays : 2 * arrays]
    send_sem, recv_sem, own_sem = refs[2 * arrays :]
    owner, core = lax.axis_index("owner"), lax.axis_index("dp")
    line, place = owner // along, owner % along
    cores = lax.axis_size("dp")

    def index(a, b, c):
        return (a * along + b) * cores + c

    line_peers = [lax.rem(line + s, lines) for s in range(1, lines)]
    row_peers = [lax.rem(place + s, along) for s in range(1, along)]
    core_peers = [lax.rem(core + s, cores) for s in range(1, cores)]
    peers = [(a, place, core) for a in line_peers]
    peers += [(line, b, core) for b in row_peers]
    peers += [(line, place, c) for c in core_peers]

    def device(a, b, c):
        return {"owner": a * along + b, "dp": c}

    barrier = pltpu.get_barrier_semaphore()
    for peer in peers:
        pl.semaphore_signal(
            barrier, inc=1, device_id=device(*peer), device_id_type=pl.DeviceIdType.MESH
        )
    pl.semaphore_wait(barrier, len(peers))

    sent = []

    def push(sources, slot, peer):
        for n in range(arrays):
            copy = pltpu.make_async_remote_copy(
                src_ref=sources[n],
                dst_ref=alls[n].at[slot],
                send_sem=send_sem.at[len(sent)],
                recv_sem=recv_sem.at[n, slot],
                device_id=device(*peer),
                device_id_type=pl.DeviceIdType.MESH,
            )
            copy.start()
            sent.append(copy)

    def arrived(slot):
        for n in range(arrays):
            pltpu.make_async_copy(blocks[n], alls[n].at[slot], recv_sem.at[n, slot]).wait()

    def held(slot):
        return [whole.at[slot] for whole in alls]

    mine = index(line, place, core)
    for peer in peers:
        push(blocks, mine, peer)
    own = [
        pltpu.make_async_copy(blocks[n], alls[n].at[mine], own_sem.at[n]) for n in range(arrays)
    ]
    for copy in own:
        copy.start()
    for a in line_peers:
        slot = index(a, place, core)
        arrived(slot)
        for b in row_peers:
            push(held(slot), slot, (line, b, core))
        for c in core_peers:
            push(held(slot), slot, (line, place, c))
    for a in [line] + line_peers:
        for b in row_peers:
            slot = index(a, b, core)
            arrived(slot)
            for c in core_peers:
                push(held(slot), slot, (line, place, c))
    for c in core_peers:
        for a in [line] + line_peers:
            for b in [place] + row_peers:
                arrived(index(a, b, c))
    for copy in own:
        copy.wait()
    for copy in sent:
        copy.wait_send()


def gather_blocks(blocks, collective_id):
    owners, cores = lax.axis_size("owner"), lax.axis_size("dp")
    along = 2 if owners < 16 else 8
    lines = owners // along
    arrays = len(blocks)
    copies = lines + along + cores - 3
    copies += (lines - 1) * (along + cores - 2) + lines * (along - 1) * (cores - 1)
    return pl.pallas_call(
        functools.partial(gather_kernel, lines, along, arrays),
        in_specs=[pl.BlockSpec(memory_space=pl.ANY)] * arrays,
        out_specs=[pl.BlockSpec(memory_space=pl.ANY)] * arrays,
        out_shape=[
            jax.ShapeDtypeStruct((owners * cores,) + block.shape, block.dtype) for block in blocks
        ],
        scratch_shapes=[
            pltpu.SemaphoreType.DMA((arrays * copies,)),
            pltpu.SemaphoreType.DMA((arrays, owners * cores)),
            pltpu.SemaphoreType.DMA((arrays,)),
        ],
        compiler_params=pltpu.CompilerParams(
            collective_id=collective_id, has_side_effects=True
        ),
        cost_estimate=pl.CostEstimate(
            flops=0,
            bytes_accessed=4 * owners * cores * sum(block.size for block in blocks),
            transcendentals=0,
        ),
    )(*blocks)


def exchange_blocks(block):
    owners, cores = lax.axis_size("owner"), lax.axis_size("dp")
    count = owners * cores
    place = jnp.arange(count, dtype=jnp.int32)
    if count > 32:
        return lax.all_gather(block, BOTH, axis=0), place
    quad = 4
    far = count // quad
    pieces = [block]
    for s in range(1, quad):
        pairs = [(i, i // quad * quad + (i + s) % quad) for i in range(count)]
        pieces.append(lax.ppermute(block, BOTH, pairs))
    near = jnp.stack(pieces)
    groups = [near]
    for s in range(1, far):
        pairs = [(i, (i + quad * s) % count) for i in range(count)]
        groups.append(lax.ppermute(near, BOTH, pairs))
    me = lax.axis_index("owner") * cores + lax.axis_index("dp")
    order = (me // quad - place // quad + far) % far * quad + (me - place + count) % quad
    return jnp.concatenate(groups, axis=0), order


def score_kernel(rollouts, per, order_ref, *refs):
    out_refs = refs[:per]
    sel_out_ref, eig_ref, masked_ref, sel_in_ref, acc_ref = refs[per:]

    @pl.when(pl.program_id(0) == 0)
    def _():
        acc_ref[...] = jnp.zeros_like(acc_ref)

    rows = eig_ref.shape[0]
    wide = sel_in_ref.shape[1]
    damped = eig_ref[...].astype(jnp.float32) + DAMPING
    rough = pl.reciprocal(damped, approx=True)
    inv = rough * (2.0 - damped * rough)
    tokens_t = jnp.concatenate([ref[0].T for ref in out_refs], axis=0)
    sel_out = sel_out_ref[...].astype(jnp.float32)
    for e in range(rollouts):
        outer = jnp.dot(tokens_t, masked_ref[e], preferred_element_type=jnp.float32)
        scaled = (outer * inv).astype(jnp.bfloat16)
        turned = jnp.dot(scaled, sel_in_ref[...], preferred_element_type=jnp.float32)
        acc_ref[e] += jnp.sum((turned * sel_out).reshape(rows // 8, 8, wide), axis=0)


def plane_scores(order, rot_out, sel_out_t, eigvals, masked_in, sel_in_t):
    total, columns = eigvals.shape
    rollouts, tokens, _ = masked_in.shape
    wide = sel_in_t.shape[1]
    block = rot_out.shape[2]
    per = max(1, 1024 // block)
    rows = per * block

    def rotated(n):
        return pl.BlockSpec((1, tokens, block), lambda i, order: (order[i * per + n], 0, 0))

    return pl.pallas_call(
        functools.partial(score_kernel, rollouts, per),
        grid_spec=pltpu.PrefetchScalarGridSpec(
            num_scalar_prefetch=1,
            grid=(total // rows,),
            in_specs=[rotated(n) for n in range(per)]
            + [
                pl.BlockSpec((rows, wide), lambda i, order: (i, 0)),
                pl.BlockSpec((rows, columns), lambda i, order: (i, 0)),
                pl.BlockSpec((rollouts, tokens, columns), lambda i, order: (0, 0, 0)),
                pl.BlockSpec((columns, wide), lambda i, order: (0, 0)),
            ],
            out_specs=pl.BlockSpec((rollouts, 8, wide), lambda i, order: (0, 0, 0)),
        ),
        out_shape=jax.ShapeDtypeStruct((rollouts, 8, wide), jnp.float32),
        compiler_params=pltpu.CompilerParams(vmem_limit_bytes=56 * 1024 * 1024),
        cost_estimate=pl.CostEstimate(
            flops=2 * rollouts * total * columns * (wide + 256),
            bytes_accessed=2 * total * (columns + wide),
            transcendentals=total * columns,
        ),
    )(order, *[rot_out] * per, sel_out_t, eigvals, masked_in, sel_in_t)


def on_device(
    activations,
    out_grads,
    lengths,
    rollout_ids,
    basis_in,
    basis_out,
    eigvals,
    query_out,
    query_in,
    query_ids,
):
    queries = query_ids.shape[0]
    bank, rank, _ = query_out.shape
    slots = activations.shape[1]
    owners = lax.axis_size("owner")
    replicas = lax.axis_size("dp")
    per_replica = lengths.shape[1]
    rollouts = rollout_ids.shape[0]
    tokens = owners * replicas * slots
    picker = (query_ids[:, None] == jnp.arange(bank, dtype=jnp.int32)[None, :]).astype(jnp.bfloat16)

    wide_in, wide_out = activations.shape[2], out_grads.shape[2]
    sel_out_t = jnp.einsum(
        "qb,brj->jqr", picker, query_out, preferred_element_type=jnp.float32
    ).astype(jnp.bfloat16)
    sel_out_t = lax.all_gather(sel_out_t.reshape(-1, queries * rank), BOTH, axis=0, tiled=True)
    sel_in_t = jnp.einsum(
        "qb,brk->kqr", picker, query_in, preferred_element_type=jnp.float32
    ).astype(jnp.bfloat16)
    sel_in_t = sel_in_t.reshape(-1, queries * rank)

    acts, grads = gather_blocks([activations.reshape(-1, 128), out_grads.reshape(-1, 128)], 0)
    acts = acts.reshape(tokens, wide_in)
    grads = grads.reshape(tokens, wide_out)
    block_out = jnp.dot(grads, basis_out, preferred_element_type=jnp.float32).astype(jnp.bfloat16)
    rot_out, order = exchange_blocks(block_out)
    rot_in = jnp.dot(acts, basis_in, preferred_element_type=jnp.float32).astype(jnp.bfloat16)

    token = jnp.arange(tokens, dtype=jnp.int32)
    place = (token // (replicas * slots)) * slots + token % slots
    replica = (token // slots) % replicas
    ends = jnp.cumsum(lengths, axis=1)
    starts = ends - lengths
    member = (
        (jnp.arange(replicas, dtype=jnp.int32)[:, None, None] == replica[None, None, :])
        & (place[None, None, :] >= starts[:, :, None])
        & (place[None, None, :] < ends[:, :, None])
    ).reshape(rollouts, tokens)
    masked_in = jnp.where(member[:, :, None], rot_in[None], jnp.zeros((), rot_in.dtype))

    acc = plane_scores(order, rot_out, sel_out_t, eigvals, masked_in, sel_in_t)
    scores = jnp.sum(acc.reshape(rollouts, 8, queries, rank), axis=(1, 3))
    shares = gather_blocks([jnp.pad(scores, ((0, 0), (0, -queries % 128)))], 1)[0]
    scores = jnp.sum(shares, axis=0)[:, :queries]
    placing = (rollout_ids[:, None] == jnp.arange(rollouts, dtype=jnp.int32)[None, :]).astype(
        jnp.float32
    )
    return jnp.sum(placing[:, :, None] * scores[:, None, :], axis=0)


def solution(mesh):
    return jax.shard_map(
        on_device,
        mesh=mesh,
        in_specs=(
            P(("groups", "dp"), "owner", None),
            P(("groups", "dp"), "owner", None),
            P("groups", None),
            P("groups"),
            P(None, BOTH),
            P(None, BOTH),
            P(None, BOTH),
            P(None, None, BOTH),
            P(None, None, BOTH),
            P("groups"),
        ),
        out_specs=P("groups", None),
        check_vma=False,
    )
```

time: 202 us -> 203 us (level)
  Pallas kernels: 140 us -> 123 us
  starting transfers between devices: 0.03 us -> 11.6 us
  waiting for transfers between devices: 0.04 us -> 6.31 us
  local copies, waits for them, and re-layouts: 13.7 us -> 11.3 us
    pallas_call x4 -> x3, Pallas kernels: 140 us -> 123 us  [the longest x1 77.3 us: plane_scores(): pl.pallas_call(functools.partial(score_kernel, rollouts, per), grid_spec=...]
    ppermute x0 -> x6, starting transfers between devices: none -> 11.6 us  [the longest x3 9.07 us: exchange_blocks(): groups.append(lax.ppermute(near, BOTH, pairs))]
    ppermute x0 -> x6, waiting for transfers between devices: none -> 6.27 us  [the longest x3 6.27 us: exchange_blocks(): groups.append(lax.ppermute(near, BOTH, pairs))]
    slice x3 -> x0, local copies, waits for them, and re-layouts: 2.95 us -> none  [the longest x1 2.94 us: on_device(): acts = gathered[:, :split].reshape(tokens, wide_in)]
    transpose x1 -> x0, local copies, waits for them, and re-layouts: 2.67 us -> none  [on_device(): gather_blocks(block_out, 1).transpose(0, 2, 1).reshape(-1, tokens)]
  transfers between devices with their start and end apart: 1 -> 7, of which waited for: 0 -> 2; matrix products, arithmetic and copies ran while one was open for 20% -> 20% of each run, Pallas kernels for 25% -> 16%
where the time goes in v3:
time: 203 us; the launch traced here: 202 us
  Pallas kernels  123 us (61%)
  matrix products  31.9 us (16%)
  between operations  13.6 us (7%)
  starting transfers between devices  11.6 us (6%)
  local copies, waits for them, and re-layouts  11.3 us (6%)
  waiting for transfers between devices  6.31 us (3%)
  other arithmetic  4.32 us (2%)
    pallas_call x1, Pallas kernels, plane_scores(): pl.pallas_call(functools.partial(score_kernel, rollouts, per), grid_spec=...  77.3 us
    pallas_call x2, Pallas kernels, gather_blocks(): pl.pallas_call(functools.partial(gather_kernel, lines, along, arrays), in...  45.9 us
    dot_general x1, matrix products, on_device(): jnp.dot(acts, basis_in, preferred_element_type=jnp.float32)  22.5 us
    ppermute x3, starting transfers between devices, exchange_blocks(): groups.append(lax.ppermute(near, BOTH, pairs))  9.07 us
    ppermute x3, waiting for transfers between devices, exchange_blocks(): groups.append(lax.ppermute(near, BOTH, pairs))  6.27 us
    dot_general x1, matrix products, on_device(): jnp.dot(grads, basis_out, preferred_element_type=jnp.float32)  4.91 us
  transfers between devices with their start and end apart: 7, of which 2 were waited for; matrix products, arithmetic and copies ran while one was open for 20% of the time, Pallas kernels for 16%

profile of v3, /device:TPU:0, one launch (start us, length us, event | category | flops | bytes accessed | tf_op | source)
XLA Modules:
  0.0 202.3 jit_solution(16336280446547799588)
XLA Ops:
  6.5 0.0 copy-start
  6.5 0.0 all-gather.2.cloned.1.call-start
  6.5 2.1 %fusion.8 = bf16[512,32,8]{0,1,2:T(8,128)(2,1)S(1)} fusion(bf16[128,8,512]{2,1,0:T(8,128)(2,1)} %param.17, s32[32]{0:T(128)} %param.19), kind=kOutput, calls=%fused_computation.5 | convolution fusion | flops 33689600 | bytes 1310848 | tf_op jit(solution)/shard_map/qb,brj->jqr/dot_general | solution.py:226
  8.7 0.2 copy.38
  8.8 0.8 copy.23
  9.7 0.0 all-gather.2.cloned.1.call-update
  9.7 1.6 reshape.159.refs_0_
  11.3 1.4 reshape.160.refs_1_
  12.7 32.9 %shard_map.100 = (bf16[16,448,128]{2,1,0:T(8,128)(2,1)}, bf16[16,128,128]{2,1,0:T(8,128)(2,1)}) custom-call(bf16[448,128]{1,0:T(8,128)(2,1)} %reshape.159.refs_0_, bf16[128,128]{1,0:T(8,128)(2,1)} %reshape.160.refs_1_), custom_call_target="tpu_custom_call" | custom-call | bytes 4718592 | tf_op jit(solution)/shard_map/pallas_call | solution.py:101
  45.7 1.4 reshape.161
  47.0 0.0 copy-start.2
  47.0 0.0 copy-start.5
  47.1 4.9 %constant_dynamic-update-slice_fusion.6 = (bf16[16,32,512]{2,1,0:T(8,128)(2,1)S(1)}, bf16[32,512]{1,0:T(8,128)(2,1)S(1)}) fusion(bf16[32,8192]{1,0:T(8,128)(2,1)S(1)} %reshape.161, bf16[8192,512]{1,0:T(8,128)(2,1)} %param.15), kind=kOutput, calls=%fused_computation.20 | convolution fusion | flops 268451840 | bytes 8978432 | tf_op jit(solution)/shard_map/dot_general | solution.py:238
  52.0 0.5 collective-permute-start
  52.5 0.8 collective-permute-start.1
  53.3 1.3 collective-permute-start.2
  54.5 0.0 copy-done.2
  54.5 0.2 reduce_window_sum.11
  54.7 0.1 lt.43
  54.8 0.1 ge.22
  54.9 2.9 %reshape.163 = bf16[32,28672]{1,0:T(8,128)(2,1)} reshape(bf16[16,448,128]{2,1,0:T(8,128)(2,1)} %get-tuple-element.8) | data formatting | bytes 3670016 | tf_op jit(solution)/shard_map/reshape | solution.py:236
  57.8 0.1 compare_and_fusion
  57.9 0.0 copy-done.5
  57.9 0.1 fusion.15
  58.0 0.0 copy-start.4
  58.0 22.5 %convolution_convert_fusion.1 = bf16[32,1024]{1,0:T(8,128)(2,1)S(1)} fusion(bf16[32,28672]{1,0:T(8,128)(2,1)} %reshape.163, bf16[28672,1024]{1,0:T(8,128)(2,1)} %param.14), kind=kOutput, calls=%fused_computation.6 | convolution fusion | flops 1879080960 | bytes 60620800 | tf_op jit(solution)/shard_map/dot_general | solution.py:240
  80.5 0.9 broadcast_select_fusion.refs_4_
  81.4 0.0 copy-done
  81.4 0.0 copy-done.4
  81.4 2.4 %fusion.5 = bf16[1024,32,8]{0,1,2:T(8,128)(2,1)S(1)} fusion(bf16[128,8,1024]{2,1,0:T(8,128)(2,1)S(1)} %copy-done, s32[32]{0:T(128)S(1)} %copy-done.4), kind=kOutput, calls=%fused_computation.3 | convolution fusion | flops 67375104 | bytes 2621568 | tf_op jit(solution)/shard_map/qb,brk->kqr/dot_general | solution.py:230
  83.8 0.5 fusion.17.order_ref
  84.4 0.3 copy.37
  84.7 1.0 copy.26.refs_5_
  85.7 0.0 collective-permute-done
  85.7 0.0 collective-permute-done.1
  85.7 0.0 collective-permute-done.2
  85.7 6.6 %collective-permute-start.3 = (bf16[4,32,512]{2,1,0:T(8,128)(2,1)S(1)}, bf16[4,32,512]{2,1,0:T(8,128)(2,1)S(1)}, u32[]{:S(2)}, u32[]{:S(2)}) collective-permute-start(bf16[4,32,512]{2,1,0:T(8,128)(2,1)S(1)} %pad_maximum_fusion), channel_id=1, source_target_pairs={{0,4},{1,5},{2,6},{3,7},{4,8},{5,9},{6,10},{7,11},{8,12},{9,13},{1... | collective-permute-start | bytes 393224 | tf_op jit(solution)/shard_map/ppermute | solution.py:140
  92.4 0.0 collective-permute-start.4
  92.4 2.4 %collective-permute-start.5 = (bf16[4,32,512]{2,1,0:T(8,128)(2,1)S(1)}, bf16[4,32,512]{2,1,0:T(8,128)(2,1)S(1)}, u32[]{:S(2)}, u32[]{:S(2)}) collective-permute-start(bf16[4,32,512]{2,1,0:T(8,128)(2,1)S(1)} %pad_maximum_fusion), channel_id=1, source_target_pairs={{0,12},{1,13},{2,14},{3,15},{4,0},{5,1},{6,2},{7,3},{8,4},{9,5},{1... | collective-permute-start | bytes 393224 | tf_op jit(solution)/shard_map/ppermute | solution.py:140
  94.8 1.4 collective-permute-done.3
  96.3 4.8 %collective-permute-done.4 = bf16[4,32,512]{2,1,0:T(8,128)(2,1)S(1)} collective-permute-done((bf16[4,32,512]{2,1,0:T(8,128)(2,1)S(1)}, bf16[4,32,512]{2,1,0:T(8,128)(2,1)S(1)}, u32[]{:S(2)}, u32[]{:S(2)}) %collective-permute-start.4) | collective-permute-done | bytes 131104 | tf_op jit(solution)/shard_map/ppermute | solution.py:140
  101.1 0.0 collective-permute-done.5
  101.1 0.0 copy-start.3
  101.1 0.0 all-gather.2.cloned.1.call-done.refs_2_
  101.2 0.8 copy-done.3
  101.9 0.0 copy-start.1
  101.9 77.3 %shard_map.101 = f32[8,8,256]{2,1,0:T(8,128)} custom-call(s32[16]{0:T(128)} %fusion.17.order_ref, bf16[16,32,512]{2,1,0:T(8,128)(2,1)} %copy-done.3, bf16[16,32,512]{2,1,0:T(8,128)(2,1)} %copy-done.3, bf16[8192,256]{1,0:T(8,128)(2,1)} %all-gather.2.cloned.1.call-done.refs_2_, bf16[8192,1024]{1,0:T(8,128)(2,1)} %refs_3_.1, ...), custom_call_target="tpu_custom_call" | custom-call | flops 68719476736 | bytes 20971520 | tf_op jit(solution)/shard_map/pallas_call | solution.py:179
  179.3 0.9 reduce_sum.34
  180.1 0.1 reduce_sum.35
  180.2 0.1 reduce_sum.36
  180.4 0.6 pad.4.refs_0_
  181.0 13.0 %shard_map.102 = f32[16,8,128]{2,1,0:T(8,128)} custom-call(f32[8,128]{1,0:T(8,128)} %pad.4.refs_0_), custom_call_target="tpu_custom_call" | custom-call | bytes 65536 | tf_op jit(solution)/shard_map/pallas_call | solution.py:101
  194.0 0.9 reduce_sum.37
  194.8 0.7 multiply_reduce_fusion
  195.5 0.0 copy-done.1
  (12 shorter events, 0.1 us)
Async XLA Ops:
  6.5 74.9 %copy-start = (bf16[128,8,1024]{2,1,0:T(8,128)(2,1)S(1)}, bf16[128,8,1024]{2,1,0:T(8,128)(2,1)}, u32[]{:S(2)}) copy-start(bf16[128,8,1024]{2,1,0:T(8,128)(2,1)} %param.18) | copy-start | bytes 6291460
  6.5 94.6 %all-gather.2.cloned.1.call-start = ((), (), s32[]{:S(2)}) async-start(), calls=%async_computation | async-start | bytes 4456448 | tf_op jit(solution)/shard_map/all_gather | solution.py:229
  47.0 7.5 %copy-start.2 = (s32[2,4]{1,0:T(2,128)S(1)}, s32[2,4]{1,0:T(2,128)}, u32[]{:S(2)}) copy-start(s32[2,4]{1,0:T(2,128)} %param.12) | copy-start | bytes 100
  47.0 10.9 %copy-start.5 = (s32[8]{0:T(128)S(1)}, s32[8]{0:T(128)}, u32[]{:S(2)}) copy-start(s32[8]{0:T(128)} %param.13) | copy-start | bytes 100
  52.0 33.7 %collective-permute-start = (bf16[32,512]{1,0:T(8,128)(2,1)S(1)}, bf16[32,512]{1,0:T(8,128)(2,1)S(1)}, u32[]{:S(2)}, u32[]{:S(2)}) collective-permute-start(bf16[32,512]{1,0:T(8,128)(2,1)S(1)} %get-tuple-element.10), channel_id=1, source_target_pairs={{0,1},{1,2},{2,3},{3,0},{4,5},{5,6},{6,7},{7,4},{8,9},{9,10},{10,1... | collective-permute-start | bytes 98312 | tf_op jit(solution)/shard_map/ppermute | solution.py:135
  52.5 33.2 %collective-permute-start.1 = (bf16[32,512]{1,0:T(8,128)(2,1)S(1)}, bf16[32,512]{1,0:T(8,128)(2,1)S(1)}, u32[]{:S(2)}, u32[]{:S(2)}) collective-permute-start(bf16[32,512]{1,0:T(8,128)(2,1)S(1)} %get-tuple-element.10), channel_id=1, source_target_pairs={{0,2},{1,3},{2,0},{3,1},{4,6},{5,7},{6,4},{7,5},{8,10},{9,11},{10,... | collective-permute-start | bytes 98312 | tf_op jit(solution)/shard_map/ppermute | solution.py:135
  53.3 32.4 %collective-permute-start.2 = (bf16[32,512]{1,0:T(8,128)(2,1)S(1)}, bf16[32,512]{1,0:T(8,128)(2,1)S(1)}, u32[]{:S(2)}, u32[]{:S(2)}) collective-permute-start(bf16[32,512]{1,0:T(8,128)(2,1)S(1)} %get-tuple-element.10), channel_id=1, source_target_pairs={{0,3},{1,0},{2,1},{3,2},{4,7},{5,4},{6,5},{7,6},{8,11},{9,8},{10,9... | collective-permute-start | bytes 98312 | tf_op jit(solution)/shard_map/ppermute | solution.py:135
  58.0 23.4 %copy-start.4 = (s32[32]{0:T(128)S(1)}, s32[32]{0:T(128)}, u32[]{:S(2)}) copy-start(s32[32]{0:T(128)} %param.19) | copy-start | bytes 388
  85.7 10.5 %collective-permute-start.3 = (bf16[4,32,512]{2,1,0:T(8,128)(2,1)S(1)}, bf16[4,32,512]{2,1,0:T(8,128)(2,1)S(1)}, u32[]{:S(2)}, u32[]{:S(2)}) collective-permute-start(bf16[4,32,512]{2,1,0:T(8,128)(2,1)S(1)} %pad_maximum_fusion), channel_id=1, source_target_pairs={{0,4},{1,5},{2,6},{3,7},{4,8},{5,9},{6,10},{7,11},{8,12},{9,13},{1... | collective-permute-start | bytes 393224 | tf_op jit(solution)/shard_map/ppermute | solution.py:140
  92.4 8.7 %collective-permute-start.4 = (bf16[4,32,512]{2,1,0:T(8,128)(2,1)S(1)}, bf16[4,32,512]{2,1,0:T(8,128)(2,1)S(1)}, u32[]{:S(2)}, u32[]{:S(2)}) collective-permute-start(bf16[4,32,512]{2,1,0:T(8,128)(2,1)S(1)} %pad_maximum_fusion), channel_id=1, source_target_pairs={{0,8},{1,9},{2,10},{3,11},{4,12},{5,13},{6,14},{7,15},{8,0},{9,1},... | collective-permute-start | bytes 393224 | tf_op jit(solution)/shard_map/ppermute | solution.py:140
  92.4 8.7 %collective-permute-start.5 = (bf16[4,32,512]{2,1,0:T(8,128)(2,1)S(1)}, bf16[4,32,512]{2,1,0:T(8,128)(2,1)S(1)}, u32[]{:S(2)}, u32[]{:S(2)}) collective-permute-start(bf16[4,32,512]{2,1,0:T(8,128)(2,1)S(1)} %pad_maximum_fusion), channel_id=1, source_target_pairs={{0,12},{1,13},{2,14},{3,15},{4,0},{5,1},{6,2},{7,3},{8,4},{9,5},{1... | collective-permute-start | bytes 393224 | tf_op jit(solution)/shard_map/ppermute | solution.py:140
  101.1 0.8 copy-start.3
  101.9 93.6 %copy-start.1 = (bf16[128,8,1024]{2,1,0:T(8,128)(2,1)S(1)}, bf16[128,8,1024]{2,1,0:T(8,128)(2,1)}, u32[]{:S(2)}) copy-start(bf16[128,8,1024]{2,1,0:T(8,128)(2,1)} %param.18) | copy-start | bytes 6291460
Sparse Core Ops, SparseCore 0:
  9.8 62.0 all-gather.1

commit v4 on v3

--- a/solution.py
+++ b/solution.py
@@ -121,26 +121,26 @@
     )(*blocks)
 
 
-def exchange_blocks(block):
+def exchange_blocks(block, later):
     owners, cores = lax.axis_size("owner"), lax.axis_size("dp")
     count = owners * cores
     place = jnp.arange(count, dtype=jnp.int32)
     if count > 32:
-        return lax.all_gather(block, BOTH, axis=0), place
+        return lax.all_gather(block, BOTH, axis=0), place, later
     quad = 4
     far = count // quad
     pieces = [block]
     for s in range(1, quad):
         pairs = [(i, i // quad * quad + (i + s) % quad) for i in range(count)]
         pieces.append(lax.ppermute(block, BOTH, pairs))
-    near = jnp.stack(pieces)
+    near, later = lax.optimization_barrier((jnp.stack(pieces), later))
     groups = [near]
     for s in range(1, far):
         pairs = [(i, (i + quad * s) % count) for i in range(count)]
         groups.append(lax.ppermute(near, BOTH, pairs))
     me = lax.axis_index("owner") * cores + lax.axis_index("dp")
     order = (me // quad - place // quad + far) % far * quad + (me - place + count) % quad
-    return jnp.concatenate(groups, axis=0), order
+    return jnp.concatenate(groups, axis=0), order, later
 
 
 def score_kernel(rollouts, per, order_ref, *refs):
@@ -236,7 +236,7 @@
     acts = acts.reshape(tokens, wide_in)
     grads = grads.reshape(tokens, wide_out)
     block_out = jnp.dot(grads, basis_out, preferred_element_type=jnp.float32).astype(jnp.bfloat16)
-    rot_out, order = exchange_blocks(block_out)
+    rot_out, order, acts = exchange_blocks(block_out, acts)
     rot_in = jnp.dot(acts, basis_in, preferred_element_type=jnp.float32).astype(jnp.bfloat16)
 
     token = jnp.arange(tokens, dtype=jnp.int32)

time: 203 us -> 193 us (0.951)
  waiting for transfers between devices: 6.31 us -> 0.03 us
    ppermute x3, waiting for transfers between devices: 6.27 us -> 0.01 us  [exchange_blocks(): groups.append(lax.ppermute(near, BOTH, pairs))]
    pallas_call x2, Pallas kernels: 45.9 us -> 43.6 us  [gather_blocks(): pl.pallas_call(functools.partial(gather_kernel, lines, along, arrays), in...]
  transfers between devices with their start and end apart: 7 -> 7, of which waited for: 2 -> 0; matrix products, arithmetic and copies ran while one was open for 20% -> 21% of each run, Pallas kernels for 16% -> 17%
where the time goes in v4:
time: 193 us; the launch traced here: 192 us
  Pallas kernels  121 us (63%)
  matrix products  31.1 us (16%)
  between operations  13.5 us (7%)
  starting transfers between devices  11.8 us (6%)
  local copies, waits for them, and re-layouts  9.53 us (5%)
  other arithmetic  5.17 us (3%)
    pallas_call x1, Pallas kernels, plane_scores(): pl.pallas_call(functools.partial(score_kernel, rollouts, per), grid_spec=...  77.3 us
    pallas_call x2, Pallas kernels, gather_blocks(): pl.pallas_call(functools.partial(gather_kernel, lines, along, arrays), in...  43.6 us
    dot_general x1, matrix products, on_device(): jnp.dot(acts, basis_in, preferred_element_type=jnp.float32)  21.7 us
    ppermute x3, starting transfers between devices, exchange_blocks(): groups.append(lax.ppermute(near, BOTH, pairs))  9.27 us
    dot_general x1, matrix products, on_device(): jnp.dot(grads, basis_out, preferred_element_type=jnp.float32)  4.91 us
  transfers between devices with their start and end apart: 7, of which 0 were waited for; matrix products, arithmetic and copies ran while one was open for 21% of the time, Pallas kernels for 17%

profile of v4, /device:TPU:0, one launch (start us, length us, event | category | flops | bytes accessed | tf_op | source)
XLA Modules:
  0.0 192.1 jit_solution(5029593725883722631)
XLA Ops:
  6.5 0.0 copy-start
  6.5 0.0 all-gather.2.cloned.1.call-start
  6.5 2.1 %fusion.8 = bf16[512,32,8]{0,1,2:T(8,128)(2,1)S(1)} fusion(bf16[128,8,512]{2,1,0:T(8,128)(2,1)} %param.17, s32[32]{0:T(128)} %param.19), kind=kOutput, calls=%fused_computation.5 | convolution fusion | flops 33689600 | bytes 1310848 | tf_op jit(solution)/shard_map/qb,brj->jqr/dot_general | solution.py:226
  8.7 0.2 copy.38
  8.8 0.8 copy.23
  9.7 0.0 all-gather.2.cloned.1.call-update
  9.7 1.6 reshape.159.refs_0_
  11.3 1.4 reshape.160.refs_1_
  12.7 32.9 %shard_map.100 = (bf16[16,448,128]{2,1,0:T(8,128)(2,1)}, bf16[16,128,128]{2,1,0:T(8,128)(2,1)}) custom-call(bf16[448,128]{1,0:T(8,128)(2,1)} %reshape.159.refs_0_, bf16[128,128]{1,0:T(8,128)(2,1)} %reshape.160.refs_1_), custom_call_target="tpu_custom_call" | custom-call | bytes 4718592 | tf_op jit(solution)/shard_map/pallas_call | solution.py:101
  45.7 1.3 reshape.161
  47.0 0.0 copy-start.2
  47.0 0.0 copy-start.4
  47.0 0.0 copy-start.3
  47.0 4.9 %convolution_convert_fusion.2 = bf16[32,512]{1,0:T(8,128)(2,1)S(1)} fusion(bf16[32,8192]{1,0:T(8,128)(2,1)S(1)} %reshape.161, bf16[8192,512]{1,0:T(8,128)(2,1)} %param.15), kind=kOutput, calls=%fused_computation.7 | convolution fusion | flops 268451840 | bytes 8945664 | tf_op jit(solution)/shard_map/dot_general | solution.py:238
  51.9 0.5 collective-permute-start
  52.4 0.8 collective-permute-start.1
  53.2 1.3 collective-permute-start.2
  54.5 0.0 copy-done.2
  54.5 0.2 reduce_window_sum.11
  54.7 0.1 lt.43
  54.8 0.1 ge.22
  54.9 0.1 compare_and_fusion
  55.0 0.0 copy-done.4
  55.0 0.1 fusion.15
  55.0 0.0 copy-done
  55.0 0.0 copy-done.3
  55.1 2.4 %fusion.5 = bf16[1024,32,8]{0,1,2:T(8,128)(2,1)S(1)} fusion(bf16[128,8,1024]{2,1,0:T(8,128)(2,1)S(1)} %copy-done, s32[32]{0:T(128)S(1)} %copy-done.3), kind=kOutput, calls=%fused_computation.3 | convolution fusion | flops 67375104 | bytes 2621568 | tf_op jit(solution)/shard_map/qb,brk->kqr/dot_general | solution.py:230
  57.5 0.5 fusion.17.order_ref
  58.0 2.0 %reshape.162 = bf16[32,28672]{1,0:T(8,128)(2,1)S(1)} reshape(bf16[16,448,128]{2,1,0:T(8,128)(2,1)} %get-tuple-element.10) | data formatting | bytes 3670016 | tf_op jit(solution)/shard_map/reshape | solution.py:236
  60.0 0.3 copy.37
  60.3 1.0 copy.26.refs_5_
  61.3 0.0 collective-permute-done
  61.3 0.0 collective-permute-done.1
  61.3 0.0 collective-permute-done.2
  61.3 6.8 %collective-permute-start.3 = (bf16[4,32,512]{2,1,0:T(8,128)(2,1)S(1)}, bf16[4,32,512]{2,1,0:T(8,128)(2,1)S(1)}, u32[]{:S(2)}, u32[]{:S(2)}) collective-permute-start(bf16[4,32,512]{2,1,0:T(8,128)(2,1)S(1)} %pad_maximum_fusion.1), channel_id=1, source_target_pairs={{0,4},{1,5},{2,6},{3,7},{4,8},{5,9},{6,10},{7,11},{8,12},{9,13},{1... | collective-permute-start | bytes 393224 | tf_op jit(solution)/shard_map/ppermute | solution.py:140
  68.2 0.0 collective-permute-start.4
  68.2 2.4 %collective-permute-start.5 = (bf16[4,32,512]{2,1,0:T(8,128)(2,1)S(1)}, bf16[4,32,512]{2,1,0:T(8,128)(2,1)S(1)}, u32[]{:S(2)}, u32[]{:S(2)}) collective-permute-start(bf16[4,32,512]{2,1,0:T(8,128)(2,1)S(1)} %pad_maximum_fusion.1), channel_id=1, source_target_pairs={{0,12},{1,13},{2,14},{3,15},{4,0},{5,1},{6,2},{7,3},{8,4},{9,5},{1... | collective-permute-start | bytes 393224 | tf_op jit(solution)/shard_map/ppermute | solution.py:140
  70.6 21.7 %convolution_convert_fusion.1 = bf16[32,1024]{1,0:T(8,128)(2,1)S(1)} fusion(bf16[32,28672]{1,0:T(8,128)(2,1)S(1)} %reshape.162, bf16[28672,1024]{1,0:T(8,128)(2,1)} %param.14), kind=kOutput, calls=%fused_computation.6 | convolution fusion | flops 1879080960 | bytes 60620800 | tf_op jit(solution)/shard_map/dot_general | solution.py:240
  92.3 0.9 broadcast_select_fusion.refs_4_
  93.2 0.0 collective-permute-done.3
  93.2 0.0 collective-permute-done.4
  93.2 0.0 collective-permute-done.5
  93.2 0.9 pad_maximum_fusion.refs_0_.refs_1_
  94.1 0.0 all-gather.2.cloned.1.call-done.refs_2_
  94.1 0.0 copy-start.1
  94.1 77.3 %shard_map.101 = f32[8,8,256]{2,1,0:T(8,128)} custom-call(s32[16]{0:T(128)} %fusion.17.order_ref, bf16[16,32,512]{2,1,0:T(8,128)(2,1)} %pad_maximum_fusion.refs_0_.refs_1_, bf16[16,32,512]{2,1,0:T(8,128)(2,1)} %pad_maximum_fusion.refs_0_.refs_1_, bf16[8192,256]{1,0:T(8,128)(2,1)} %all-gather.2.cloned.1.call-done.refs_2_, bf16[8192,1024]{1,0:T(8,128)(2,1)} %refs_3_.1, ...), custom_call_target="tpu_custom_call" | custom-call | flops 68719476736 | bytes 20971520 | tf_op jit(solution)/shard_map/pallas_call | solution.py:179
  171.4 0.9 reduce_sum.34
  172.3 0.1 reduce_sum.35
  172.4 0.1 reduce_sum.36
  172.5 0.6 pad.4.refs_0_
  173.1 10.6 %shard_map.102 = f32[16,8,128]{2,1,0:T(8,128)} custom-call(f32[8,128]{1,0:T(8,128)} %pad.4.refs_0_), custom_call_target="tpu_custom_call" | custom-call | bytes 65536 | tf_op jit(solution)/shard_map/pallas_call | solution.py:101
  183.7 0.9 reduce_sum.37
  184.6 0.7 multiply_reduce_fusion
  185.3 0.0 copy-done.1
  (6 shorter events, 0.1 us)
Async XLA Ops:
  6.5 48.5 %copy-start = (bf16[128,8,1024]{2,1,0:T(8,128)(2,1)S(1)}, bf16[128,8,1024]{2,1,0:T(8,128)(2,1)}, u32[]{:S(2)}) copy-start(bf16[128,8,1024]{2,1,0:T(8,128)(2,1)} %param.18) | copy-start | bytes 6291460
  6.5 87.5 %all-gather.2.cloned.1.call-start = ((), (), s32[]{:S(2)}) async-start(), calls=%async_computation | async-start | bytes 4456448 | tf_op jit(solution)/shard_map/all_gather | solution.py:229
  47.0 7.5 %copy-start.2 = (s32[2,4]{1,0:T(2,128)S(1)}, s32[2,4]{1,0:T(2,128)}, u32[]{:S(2)}) copy-start(s32[2,4]{1,0:T(2,128)} %param.12) | copy-start | bytes 100
  47.0 8.0 %copy-start.4 = (s32[8]{0:T(128)S(1)}, s32[8]{0:T(128)}, u32[]{:S(2)}) copy-start(s32[8]{0:T(128)} %param.13) | copy-start | bytes 100
  47.0 8.0 %copy-start.3 = (s32[32]{0:T(128)S(1)}, s32[32]{0:T(128)}, u32[]{:S(2)}) copy-start(s32[32]{0:T(128)} %param.19) | copy-start | bytes 388
  51.9 9.4 %collective-permute-start = (bf16[32,512]{1,0:T(8,128)(2,1)S(1)}, bf16[32,512]{1,0:T(8,128)(2,1)S(1)}, u32[]{:S(2)}, u32[]{:S(2)}) collective-permute-start(bf16[32,512]{1,0:T(8,128)(2,1)S(1)} %convolution_convert_fusion.2), channel_id=1, source_target_pairs={{0,1},{1,2},{2,3},{3,0},{4,5},{5,6},{6,7},{7,4},{8,9},{9,10},{10,1... | collective-permute-start | bytes 98312 | tf_op jit(solution)/shard_map/ppermute | solution.py:135
  52.4 8.9 %collective-permute-start.1 = (bf16[32,512]{1,0:T(8,128)(2,1)S(1)}, bf16[32,512]{1,0:T(8,128)(2,1)S(1)}, u32[]{:S(2)}, u32[]{:S(2)}) collective-permute-start(bf16[32,512]{1,0:T(8,128)(2,1)S(1)} %convolution_convert_fusion.2), channel_id=1, source_target_pairs={{0,2},{1,3},{2,0},{3,1},{4,6},{5,7},{6,4},{7,5},{8,10},{9,11},{10,... | collective-permute-start | bytes 98312 | tf_op jit(solution)/shard_map/ppermute | solution.py:135
  53.2 8.1 %collective-permute-start.2 = (bf16[32,512]{1,0:T(8,128)(2,1)S(1)}, bf16[32,512]{1,0:T(8,128)(2,1)S(1)}, u32[]{:S(2)}, u32[]{:S(2)}) collective-permute-start(bf16[32,512]{1,0:T(8,128)(2,1)S(1)} %convolution_convert_fusion.2), channel_id=1, source_target_pairs={{0,3},{1,0},{2,1},{3,2},{4,7},{5,4},{6,5},{7,6},{8,11},{9,8},{10,9... | collective-permute-start | bytes 98312 | tf_op jit(solution)/shard_map/ppermute | solution.py:135
  61.3 31.9 %collective-permute-start.3 = (bf16[4,32,512]{2,1,0:T(8,128)(2,1)S(1)}, bf16[4,32,512]{2,1,0:T(8,128)(2,1)S(1)}, u32[]{:S(2)}, u32[]{:S(2)}) collective-permute-start(bf16[4,32,512]{2,1,0:T(8,128)(2,1)S(1)} %pad_maximum_fusion.1), channel_id=1, source_target_pairs={{0,4},{1,5},{2,6},{3,7},{4,8},{5,9},{6,10},{7,11},{8,12},{9,13},{1... | collective-permute-start | bytes 393224 | tf_op jit(solution)/shard_map/ppermute | solution.py:140
  68.2 25.0 %collective-permute-start.4 = (bf16[4,32,512]{2,1,0:T(8,128)(2,1)S(1)}, bf16[4,32,512]{2,1,0:T(8,128)(2,1)S(1)}, u32[]{:S(2)}, u32[]{:S(2)}) collective-permute-start(bf16[4,32,512]{2,1,0:T(8,128)(2,1)S(1)} %pad_maximum_fusion.1), channel_id=1, source_target_pairs={{0,8},{1,9},{2,10},{3,11},{4,12},{5,13},{6,14},{7,15},{8,0},{9,1},... | collective-permute-start | bytes 393224 | tf_op jit(solution)/shard_map/ppermute | solution.py:140
  68.2 25.0 %collective-permute-start.5 = (bf16[4,32,512]{2,1,0:T(8,128)(2,1)S(1)}, bf16[4,32,512]{2,1,0:T(8,128)(2,1)S(1)}, u32[]{:S(2)}, u32[]{:S(2)}) collective-permute-start(bf16[4,32,512]{2,1,0:T(8,128)(2,1)S(1)} %pad_maximum_fusion.1), channel_id=1, source_target_pairs={{0,12},{1,13},{2,14},{3,15},{4,0},{5,1},{6,2},{7,3},{8,4},{9,5},{1... | collective-permute-start | bytes 393224 | tf_op jit(solution)/shard_map/ppermute | solution.py:140
  94.1 91.2 %copy-start.1 = (bf16[128,8,1024]{2,1,0:T(8,128)(2,1)S(1)}, bf16[128,8,1024]{2,1,0:T(8,128)(2,1)}, u32[]{:S(2)}) copy-start(bf16[128,8,1024]{2,1,0:T(8,128)(2,1)} %param.18) | copy-start | bytes 6291460
Sparse Core Ops, SparseCore 0:
  9.8 69.0 all-gather.1
